TPU v7x, 256 devices: a whole 4x4x8 slice. The times are simulated.
256 devices in a mesh: dp: 16 (over x_lo, y, core), feat: 16 (over z, x_hi).
Axes of the slice: x: 4 (x_hi: 2, x_lo: 2; x = x_hi * 2 + x_lo), y: 4, z: 8, core: 2. Of those that a mesh axis runs over, the one named last changes fastest.
Arguments:
- z_one: bfloat16 [2048, 16384], P('dp', 'feat'), may hold values from -80 to 80
- z_two: bfloat16 [2048, 16384], P('dp', 'feat'), may hold values from -80 to 80
- hidden_in: bfloat16 [2048, 16384], P('feat', 'dp'), may hold values from -6 to 6
- grad_acc: float32 [16384, 16384], P('dp', 'feat'), may hold values from -6 to 6
- loss_scale: float32 [1], replicated, may hold values from 128 to 512
Outputs:
- grad_out: float32 [16384, 16384], P('dp', 'feat')
- loss_value: float32 [1], replicated
All inputs are finite; a program needn't handle non-finite values.
Results may differ from a plain program's by a relative error of at most 0.0065.
Values may be sent and summed in bfloat16 or wider, within the bound.
A program may use at most 128 MiB of HBM per device.

v0:
```python
import jax
import jax.numpy as jnp
from jax import lax
from jax.sharding import PartitionSpec as P

off_weight = 0.0051
eps = 1e-05


def body(z_one, z_two, hidden_in, grad_acc, loss_scale):
    dp_count = lax.axis_size("dp")
    feat_count = lax.axis_size("feat")
    dp_index = lax.axis_index("dp")
    feat_index = lax.axis_index("feat")
    local_rows, local_cols = z_one.shape
    batch = local_rows * dp_count
    width = local_cols * feat_count
    values_one = z_one.astype(jnp.float32)
    values_two = z_two.astype(jnp.float32)
    totals = lax.psum(
        (
            jnp.sum(values_one, axis=0),
            jnp.sum(values_one * values_one, axis=0),
            jnp.sum(values_two, axis=0),
            jnp.sum(values_two * values_two, axis=0),
        ),
        "dp",
    )
    centre_one = totals[0] / batch
    inverse_one = lax.rsqrt(totals[1] / batch - centre_one * centre_one + eps)
    centre_two = totals[2] / batch
    inverse_two = lax.rsqrt(totals[3] / batch - centre_two * centre_two + eps)
    send_one = ((values_one - centre_one) * inverse_one).astype(jnp.bfloat16)
    send_two = ((values_two - centre_two) * inverse_two).astype(jnp.bfloat16)
    rows_all = lax.all_gather(send_one, "dp", axis=0, tiled=True)
    span = width // dp_count
    offsets = jnp.arange(span, dtype=jnp.int32)
    wide_rows = lax.all_gather(send_two, "feat", axis=1, tiled=True)
    columns = lax.all_to_all(wide_rows, "dp", split_axis=1, concat_axis=0, tiled=True)
    col_index = dp_index * span + offsets
    row_index = feat_index * local_cols + jnp.arange(local_cols, dtype=jnp.int32)
    corr = (
        lax.dot_general(
            rows_all, columns, (((0,), (0,)), ((), ())), preferred_element_type=jnp.float32
        )
        / batch
    )
    on_diag = row_index[:, None] == col_index[None, :]
    partial_loss = jnp.sum(jnp.where(on_diag, (1.0 - corr) ** 2, off_weight * corr * corr))
    loss_total = lax.psum(partial_loss, ("dp", "feat")) / width
    cotangent = (
        jnp.where(on_diag, -2.0 * (1.0 - corr), 2.0 * off_weight * corr) * (loss_scale[0] / batch)
    ).astype(jnp.bfloat16)
    grad_norm = lax.psum_scatter(
        lax.dot_general(
            columns, cotangent, (((1,), (1,)), ((), ())), preferred_element_type=jnp.float32
        ),
        "dp",
        scatter_dimension=0,
        tiled=True,
    )
    share_float = send_one.astype(jnp.float32)
    sum_grad, sum_cross = lax.psum(
        (jnp.sum(grad_norm, axis=0), jnp.sum(grad_norm * share_float, axis=0)), "dp"
    )
    grad_z = (
        (grad_norm - sum_grad / batch - share_float * (sum_cross / batch)) * inverse_one
    ).astype(jnp.bfloat16)
    hidden_all = lax.all_gather(hidden_in, "feat", axis=0, tiled=True)
    weight_grad = lax.dot_general(
        hidden_all,
        lax.all_gather(grad_z, "dp", axis=0, tiled=True),
        (((0,), (0,)), ((), ())),
        preferred_element_type=jnp.float32,
    )
    return (grad_acc + weight_grad, jnp.reshape(loss_total, (1,)))


def solution(mesh):
    placed = (P("dp", "feat"), P("dp", "feat"), P("feat", "dp"), P("dp", "feat"), P())
    return jax.shard_map(
        body, mesh=mesh, in_specs=placed, out_specs=(P("dp", "feat"), P()), check_vma=False
    )
```

profile of v0, /device:TPU:1, one launch (start us, length us, event | category | flops | bytes accessed | tf_op | source)
XLA Modules:
  0.0 507.8 jit_solution(8420432261676247474)
XLA Ops:
  7.2 0.0 all-gather.5.cloned.1.call-start
  7.2 1.1 copy.11
  8.3 0.3 convert_reduce_fusion.1
  8.6 1.0 convert_reduce_fusion
  9.7 53.2 %all-reduce.1 = (f32[1024]{0:T(1024)S(1)}, f32[1024]{0:T(1024)S(1)}, f32[1024]{0:T(1024)S(1)}, f32[1024]{0:T(1024)S(1)}) all-reduce(f32[1024]{0:T(1024)S(1)} %get-tuple-element.13, f32[1024]{0:T(1024)S(1)} %get-tuple-element.12, f32[1024]{0:T(1024)S(1)} %get-tuple-element.11, ...), channel_id=1, replica_groups=mesh['dp'=16,'feat'=16] {'dp'}, use_global_device_ids=true, to_apply=%region_7.0 | all-reduce | flops 4096 | bytes 32768 | tf_op jit(solution)/shard_map/psum | solution.py:20
  62.9 1.0 fusion.17
  63.9 0.0 all-gather.5.cloned.1.call-update
  63.9 0.0 all-gather.7.cloned.1.call-start
  64.0 1.7 fusion.20
  65.7 0.0 all-gather.7.cloned.1.call-update
  65.7 98.9 %all-gather.5.cloned.1.call-done = bf16[128,16384]{0,1:T(8,128)(2,1)} async-done(((bf16[128,1024]{0,1:T(8,128)(2,1)}), bf16[128,16384]{0,1:T(8,128)(2,1)}) %all-gather.5.cloned.1.call-update) | async-done | bytes 4194320 | tf_op jit(solution)/shard_map/all_gather | solution.py:38
  164.7 8.2 %all-to-all-start = ((bf16[128,16,1024]{0,2,1:T(8,128)(2,1)}), bf16[128,16,1024]{0,2,1:T(8,128)(2,1)}, u32[]{:S(2)}, u32[]{:S(2)}) async-start(bf16[128,16,1024]{0,2,1:T(8,128)(2,1)} %bitcast.12), calls=%async_computation | async-start | bytes 8388608 | tf_op jit(solution)/shard_map/all_to_all | solution.py:39
  172.9 0.0 reduce-scatter.2.cloned.1.call-start
  173.6 74.7 %all-to-all-done = bf16[128,16,1024]{0,2,1:T(8,128)(2,1)} async-done(((bf16[128,16,1024]{0,2,1:T(8,128)(2,1)}), bf16[128,16,1024]{0,2,1:T(8,128)(2,1)}, u32[]{:S(2)}, u32[]{:S(2)}) %all-to-all-start) | async-done | bytes 4194336 | tf_op jit(solution)/shard_map/all_to_all | solution.py:39
  248.3 6.4 %copy.12 = bf16[16,128,1024]{2,1,0:T(8,128)(2,1)} copy(bf16[16,128,1024]{1,2,0:T(8,128)(2,1)} %bitcast.1) | data formatting | bytes 8388608 | tf_op jit(solution)/shard_map/all_to_all | solution.py:39
  254.7 9.1 %fusion.2 = (f32[]{:T(128)}, f32[1024,1024]{1,0:T(8,128)S(1)}) fusion(s32[1024]{0:T(1024)S(1)} %get-tuple-element.28, s32[1024]{0:T(1024)S(1)} %get-tuple-element.29, bf16[2048,1024]{1,0:T(8,128)(2,1)} %all-gather.7.cloned.1.call-done, bf16[2048,1024]{1,0:T(8,128)(2,1)} %bitcast.13), kind=kOutput, calls=%fused_computation.4 | convolution fusion | flops 4303355904 | bytes 12591108 | tf_op jit(solution)/shard_map/dot_general | solution.py:43
  263.8 7.7 %fusion.3 = f32[2048,1024]{1,0:T(8,128)} fusion(bf16[2048,1024]{1,0:T(8,128)(2,1)S(1)} %bitcast.14, f32[1024,1024]{1,0:T(8,128)S(1)} %get-tuple-element.25, f32[]{:T(128)} %bitcast.3, s32[1024]{0:T(1024)S(1)} %get-tuple-element.28, s32[1024]{0:T(1024)S(1)} %get-tuple-element.29), kind=kOutput, calls=%fused_computation.6 | convolution fusion | flops 4303355904 | bytes 16785412 | tf_op jit(solution)/shard_map/dot_general | solution.py:55
  271.5 0.0 reduce-scatter.2.cloned.1.call-update
  271.5 0.0 all-gather.11.cloned.1.call-start
  271.6 0.5 all-gather.11.cloned.1.call-update
  272.1 0.0 all-gather.9.cloned.1.call-start
  272.1 67.3 %reduce-scatter.2.cloned.1.call-done = f32[128,1024]{1,0:T(8,128)} async-done(((f32[2048,1024]{1,0:T(8,128)}), f32[128,1024]{1,0:T(8,128)}) %reduce-scatter.2.cloned.1.call-update) | async-done | bytes 524304 | tf_op jit(solution)/shard_map/reduce_scatter | solution.py:54
  339.4 1.2 fusion.26
  340.6 31.6 %all-reduce = (f32[1024]{0:T(1024)S(1)}, f32[1024]{0:T(1024)S(1)}) all-reduce(f32[1024]{0:T(1024)S(1)} %get-tuple-element.9, f32[1024]{0:T(1024)S(1)} %get-tuple-element.8), channel_id=1, replica_groups=mesh['dp'=16,'feat'=16] {'dp'}, use_global_device_ids=true, to_apply=%region_12.13 | all-reduce | flops 2048 | bytes 16384 | tf_op jit(solution)/shard_map/psum | solution.py:63
  372.3 1.9 fusion.15
  374.1 0.0 all-gather.9.cloned.1.call-update
  374.2 5.4 %copy.13 = f32[1024,1024]{0,1:T(8,128)} copy(f32[1024,1024]{1,0:T(8,128)} %param.8) | data formatting | bytes 8388608 | tf_op args[3]
  379.5 77.0 %psum.55 = f32[]{:T(128)} all-reduce(f32[]{:T(128)} %get-tuple-element.24), channel_id=1, replica_groups=mesh['dp'=16,'feat'=16] {'dp','feat'}, use_global_device_ids=true, to_apply=%region_14.15 | all-reduce | flops 1 | bytes 8 | tf_op jit(solution)/shard_map/psum | solution.py:50
  457.2 0.0 all-gather.11.cloned.1.call-done
  457.2 26.4 %all-gather.9.cloned.1.call-done = bf16[2048,1024]{1,0:T(8,128)(2,1)} async-done(((bf16[128,1024]{1,0:T(8,128)(2,1)}), bf16[2048,1024]{1,0:T(8,128)(2,1)}) %all-gather.9.cloned.1.call-update) | async-done | bytes 4194320 | tf_op jit(solution)/shard_map/all_gather | solution.py:72
  483.6 11.2 %bitcast_add_fusion = f32[1024,1024]{0,1:T(8,128)} fusion(f32[1024,1024]{0,1:T(8,128)} %copy.13, bf16[2048,1024]{1,0:T(8,128)(2,1)} %all-gather.9.cloned.1.call-done, bf16[2048,1024]{1,0:T(8,128)(2,1)} %all-gather.11.cloned.1.call-done), kind=kOutput, calls=%fused_computation.5 | convolution fusion | flops 4296015872 | bytes 16777216 | tf_op jit(solution)/shard_map/dot_general | solution.py:70
  494.8 5.3 %copy.14 = f32[1024,1024]{1,0:T(8,128)} copy(f32[1024,1024]{0,1:T(8,128)} %bitcast_add_fusion) | data formatting | bytes 8388608
  (9 shorter events, 0.0 us)
Async XLA Ops:
  7.2 157.5 %all-gather.5.cloned.1.call-start = ((), (), s32[]{:S(2)}) async-start(), calls=%async_computation.2 | async-start | bytes 4456448 | tf_op jit(solution)/shard_map/all_gather | solution.py:38
  63.9 190.8 %all-gather.7.cloned.1.call-start = ((), (), s32[]{:S(2)}) async-start(), calls=%async_computation.3 | async-start | bytes 4456448 | tf_op jit(solution)/shard_map/all_gather | solution.py:35
  164.7 83.6 %all-to-all-start = ((bf16[128,16,1024]{0,2,1:T(8,128)(2,1)}), bf16[128,16,1024]{0,2,1:T(8,128)(2,1)}, u32[]{:S(2)}, u32[]{:S(2)}) async-start(bf16[128,16,1024]{0,2,1:T(8,128)(2,1)} %bitcast.12), calls=%async_computation | async-start | bytes 8388608 | tf_op jit(solution)/shard_map/all_to_all | solution.py:39
  172.9 166.5 %reduce-scatter.2.cloned.1.call-start = ((), (), s32[]{:S(2)}) async-start(), calls=%async_computation.4 | async-start | bytes 8912896 | tf_op jit(solution)/shard_map/reduce_scatter | solution.py:54
  254.7 9.1 %copy-start = (bf16[16,128,1024]{2,1,0:T(8,128)(2,1)S(1)}, bf16[16,128,1024]{2,1,0:T(8,128)(2,1)}, u32[]{:S(2)}) copy-start(bf16[16,128,1024]{2,1,0:T(8,128)(2,1)} %copy.12) | copy-start | bytes 12582916
  271.5 67.9 %copy-start.1 = (bf16[128,1024]{1,0:T(8,128)(2,1)S(1)}, bf16[128,1024]{1,0:T(8,128)(2,1)}, u32[]{:S(2)}) copy-start(bf16[128,1024]{1,0:T(8,128)(2,1)} %param.5) | copy-start | bytes 786436
  271.5 185.7 %all-gather.11.cloned.1.call-start = ((), (), s32[]{:S(2)}) async-start(), calls=%async_computation.6 | async-start | bytes 4456448 | tf_op jit(solution)/shard_map/all_gather | solution.py:69
  272.1 211.5 %all-gather.9.cloned.1.call-start = ((), (), s32[]{:S(2)}) async-start(), calls=%async_computation.5 | async-start | bytes 4456448 | tf_op jit(solution)/shard_map/all_gather | solution.py:72
Sparse Core Ops, SparseCore 0:
  64.1 100.5 all-gather.4
  166.5 78.7 all-gather.6
  271.6 67.7 reduce-scatter.1
  341.9 99.7 all-gather.10
  443.4 40.1 all-gather.8
where the time goes:
time: 508 us
  waiting for transfers between devices  268 us (53%)
  blocking collectives  162 us (32%)
  matrix products  28 us (6%)
  local copies, waits for them, and re-layouts  18.2 us (4%)
  between operations  16.3 us (3%)
  starting transfers between devices  8.43 us (2%)
  other arithmetic  7.16 us (1%)
    all_gather x1, waiting for transfers between devices, body(): wide_rows = lax.all_gather(send_two, 'feat', axis=1, tiled=True)  98.9 us
    psum x1, blocking collectives, body(): loss_total = lax.psum(partial_loss, ('dp', 'feat')) / width  77 us
    all_to_all x1, waiting for transfers between devices, body(): lax.all_to_all(wide_rows, 'dp', split_axis=1, concat_axis=0, tiled=True)  74.7 us
    reduce_scatter x1, waiting for transfers between devices, body(): lax.psum_scatter(lax.dot_general(columns, cotangent, (((1,), (1,)), ((),...  67.3 us
    psum x1, blocking collectives, body(): lax.psum((jnp.sum(values_one, axis=0), jnp.sum(values_one * values_one, a...  53.2 us
    psum x1, blocking collectives, body(): lax.psum((jnp.sum(grad_norm, axis=0), jnp.sum(grad_norm * share_float, ax...  31.6 us
    all_gather x1, waiting for transfers between devices, body(): lax.all_gather(grad_z, 'dp', axis=0, tiled=True)  26.4 us
    unnamed x7, local copies, waits for them, and re-layouts  11.8 us
  transfers between devices with their start and end apart: 6, of which 4 were waited for; matrix products, arithmetic and copies ran while one was open for 3% of the time, Pallas kernels for 0%

commit v1 on v0

v1 whole, which is shorter than its diff:
```python
import jax
import jax.numpy as jnp
from jax import lax
from jax.sharding import PartitionSpec as P

off_weight = 0.0051
eps = 1e-05


def standardize(raw):
    values = raw.astype(jnp.float32)
    centre = jnp.mean(values, axis=0)
    spread = jnp.mean((values - centre) ** 2, axis=0)
    inverse = lax.rsqrt(spread + eps)
    return ((values - centre) * inverse).astype(jnp.bfloat16), inverse


def body(z_one, z_two, hidden_in, grad_acc, loss_scale):
    dp_count = lax.axis_size("dp")
    feat_count = lax.axis_size("feat")
    dp_index = lax.axis_index("dp")
    local_rows, local_cols = z_one.shape
    batch = local_rows * dp_count
    width = local_cols * feat_count
    two_all = lax.all_gather(z_two, "dp", axis=0, tiled=True)
    one_all = lax.all_gather(z_one, "dp", axis=0, tiled=True)
    hidden_all = lax.all_gather(hidden_in, "feat", axis=0, tiled=True)
    normed_two, _ = standardize(two_all)
    normed_one, inverse_one = standardize(one_all)
    own_two = lax.dynamic_slice_in_dim(normed_two, dp_index * local_rows, local_rows, 0)
    own_one = lax.dynamic_slice_in_dim(normed_one, dp_index * local_rows, local_rows, 0)
    gram = lax.psum(
        lax.dot_general(
            own_two, normed_two, (((1,), (1,)), ((), ())), preferred_element_type=jnp.float32
        ),
        "feat",
    ).astype(jnp.bfloat16)
    spread = lax.dot_general(
        gram, normed_one, (((1,), (0,)), ((), ())), preferred_element_type=jnp.float32
    )
    corr_diag = (
        jnp.sum(normed_one.astype(jnp.float32) * normed_two.astype(jnp.float32), axis=0) / batch
    )
    share = own_one.astype(jnp.float32)
    scale = loss_scale[0] / batch
    weight_diag = scale * (-2.0 * (1.0 - corr_diag) - 2.0 * off_weight * corr_diag)
    grad_norm = spread * (scale * 2.0 * off_weight / batch) + own_two.astype(
        jnp.float32
    ) * weight_diag
    square_total = jnp.sum(spread * share) / (float(batch) * float(batch))
    diag_part = jnp.sum((1.0 - corr_diag) ** 2 - off_weight * corr_diag * corr_diag)
    loss_total = (
        lax.psum(off_weight * square_total + diag_part / dp_count, ("dp", "feat")) / width
    )
    sum_grad, sum_cross = lax.psum(
        (jnp.sum(grad_norm, axis=0), jnp.sum(grad_norm * share, axis=0)), "dp"
    )
    grad_z = (
        (grad_norm - sum_grad / batch - share * (sum_cross / batch)) * inverse_one
    ).astype(jnp.bfloat16)
    weight_grad = lax.dot_general(
        hidden_all,
        lax.all_gather(grad_z, "dp", axis=0, tiled=True),
        (((0,), (0,)), ((), ())),
        preferred_element_type=jnp.float32,
    )
    return (grad_acc + weight_grad, jnp.reshape(loss_total, (1,)))


def solution(mesh):
    placed = (P("dp", "feat"), P("dp", "feat"), P("feat", "dp"), P("dp", "feat"), P())
    return jax.shard_map(
        body, mesh=mesh, in_specs=placed, out_specs=(P("dp", "feat"), P()), check_vma=False
    )
```

time: 508 us -> 353 us (0.69)
  waiting for transfers between devices: 268 us -> 83.3 us
  blocking collectives: 162 us -> 204 us
  matrix products: 28 us -> 16.6 us
  other arithmetic: 7.16 us -> 17.8 us
  starting transfers between devices: 8.43 us -> 0.15 us
  local copies, waits for them, and re-layouts: 18.2 us -> 13.1 us
    all_to_all x1 -> x0, waiting for transfers between devices: 74.7 us -> none  [body(): lax.all_to_all(wide_rows, 'dp', split_axis=1, concat_axis=0, tiled=True)]
    reduce_scatter x1 -> x0, waiting for transfers between devices: 67.3 us -> none  [body(): lax.psum_scatter(lax.dot_general(columns, cotangent, (((1,), (1,)), ((),...]
    psum x3, blocking collectives: 162 us -> 204 us  [the longest x1 89.1 us: body(): lax.psum(lax.dot_general(own_two, normed_two, (((1,), (1,)), ((), ())), p...]
    all_gather x1, waiting for transfers between devices: 26.4 us -> 0.02 us  [body(): lax.all_gather(grad_z, 'dp', axis=0, tiled=True)]
    all_gather x2, waiting for transfers between devices: 98.9 us -> 81.2 us  [the longest x1 43.9 us: body(): one_all = lax.all_gather(z_one, 'dp', axis=0, tiled=True)]
    reduce_sum x3 -> x6, other arithmetic: 2.49 us -> 15.9 us  [the longest x2 6.07 us: standardize(): centre = jnp.mean(values, axis=0)]
    dot_general x2, matrix products: 16.8 us -> 5.35 us  [the longest x1 3.84 us: body(): lax.dot_general(gram, normed_one, (((1,), (0,)), ((), ())), preferred_ele...]
    all_to_all x1 -> x0, starting transfers between devices: 8.23 us -> none  [body(): lax.all_to_all(wide_rows, 'dp', split_axis=1, concat_axis=0, tiled=True)]
  transfers between devices with their start and end apart: 6 -> 4, of which waited for: 4 -> 2; matrix products, arithmetic and copies ran while one was open for 3% -> 8% of each run, Pallas kernels for 0% -> 0%
where the time goes in v1:
time: 353 us
  blocking collectives  204 us (58%)
  waiting for transfers between devices  83.3 us (24%)
  other arithmetic  17.8 us (5%)
  between operations  17.5 us (5%)
  matrix products  16.6 us (5%)
  local copies, waits for them, and re-layouts  13.1 us (4%)
    psum x1, blocking collectives, body(): lax.psum(lax.dot_general(own_two, normed_two, (((1,), (1,)), ((), ())), p...  89.1 us
    psum x1, blocking collectives, body(): lax.psum(off_weight * square_total + diag_part / dp_count, ('dp', 'feat'))  76.1 us
    all_gather x1, waiting for transfers between devices, body(): one_all = lax.all_gather(z_one, 'dp', axis=0, tiled=True)  43.9 us
    psum x1, blocking collectives, body(): lax.psum((jnp.sum(grad_norm, axis=0), jnp.sum(grad_norm * share, axis=0))...  39.2 us
    all_gather x1, waiting for transfers between devices, body(): two_all = lax.all_gather(z_two, 'dp', axis=0, tiled=True)  37.3 us
    unnamed x10, local copies, waits for them, and re-layouts  13.1 us
    dot_general x1, matrix products, body(): lax.dot_general(hidden_all, lax.all_gather(grad_z, 'dp', axis=0, tiled=Tr...  11.2 us
  transfers between devices with their start and end apart: 4, of which 2 were waited for; matrix products, arithmetic and copies ran while one was open for 8% of the time, Pallas kernels for 0%

profile of v1, /device:TPU:1, one launch (start us, length us, event | category | flops | bytes accessed | tf_op | source)
XLA Modules:
  0.0 352.8 jit_solution(7216858002715253432)
XLA Ops:
  7.2 0.0 all-gather.7.cloned.1.call-start
  7.2 0.7 all-gather.7.cloned.1.call-update
  7.9 0.0 all-gather.5.cloned.1.call-start
  7.9 0.7 all-gather.5.cloned.1.call-update
  8.6 0.0 all-gather.11.cloned.1.call-start
  8.7 0.7 all-gather.11.cloned.1.call-update
  9.4 0.0 all-gather.9.cloned.1.call-start
  10.1 43.9 %all-gather.7.cloned.1.call-done = bf16[2048,1024]{1,0:T(8,128)(2,1)} async-done(((bf16[128,1024]{1,0:T(8,128)(2,1)}), bf16[2048,1024]{1,0:T(8,128)(2,1)}) %all-gather.7.cloned.1.call-update) | async-done | bytes 4194320 | tf_op jit(solution)/shard_map/all_gather | solution.py:26
  54.0 0.0 copy-start
  54.0 3.0 convert_reduce_fusion
  57.0 0.4 copy-done
  57.4 1.1 fusion.4
  58.6 37.3 %all-gather.5.cloned.1.call-done = bf16[2048,1024]{1,0:T(8,128)(2,1)} async-done(((bf16[128,1024]{1,0:T(8,128)(2,1)}), bf16[2048,1024]{1,0:T(8,128)(2,1)}) %all-gather.5.cloned.1.call-update) | async-done | bytes 4194320 | tf_op jit(solution)/shard_map/all_gather | solution.py:25
  95.9 3.0 convert_reduce_fusion.1
  98.9 4.0 %fusion.6 = f32[1024]{0:T(1024)S(1)} fusion(bf16[2048,1024]{1,0:T(8,128)(2,1)} %all-gather.5.cloned.1.call-done, f32[1024]{0:T(1024)S(1)} %broadcast_multiply_fusion.3), kind=kLoop, calls=%fused_computation.10 | loop fusion | flops 8387584 | bytes 4202496 | tf_op jit(solution)/shard_map/reduce_sum | solution.py:13
  102.9 0.0 copy-done.1
  102.9 0.0 copy-done.2
  102.9 4.0 %multiply_reduce_fusion = (f32[1024]{0:T(1024)S(1)}, bf16[2048,1024]{1,0:T(8,128)(2,1)}, bf16[2048,1024]{1,0:T(8,128)(2,1)S(1)}) fusion(f32[1024]{0:T(1024)S(1)} %add_rsqrt_fusion, f32[1024]{0:T(1024)S(1)} %broadcast_multiply_fusion.2, bf16[2048,1024]{1,0:T(8,128)(2,1)S(1)} %copy-done.1, f32[1024]{0:T(1024)S(1)} %add_rsqrt_fusion.1, ...), kind=kLoop, calls=%fused_computation.12 | loop fusion | flops 25164800 | bytes 16797696 | tf_op jit(solution)/shard_map/reduce_sum | solution.py:42
  107.0 2.0 copy-done.3
  108.9 1.5 fusion.15
  110.4 0.6 subtract_reduce_fusion
  111.1 89.1 %all-reduce.2 = bf16[128,2048]{1,0:T(8,128)(2,1)S(1)} all-reduce(f32[128,2048]{1,0:T(8,128)S(1)} %fusion.15), channel_id=1, replica_groups=mesh['dp'=16,'feat'=16] {'feat'}, use_global_device_ids=true, to_apply=%region_2.0 | all-reduce | flops 262144 | bytes 1572864 | tf_op jit(solution)/shard_map/psum | solution.py:32
  200.1 3.8 %fusion.17 = (f32[1024]{0:T(1024)S(1)}, f32[1024]{0:T(1024)S(1)}, f32[]{:T(128)}, f32[128,1024]{1,0:T(8,128)S(1)}) fusion(f32[1024]{0:T(1024)S(1)} %get-tuple-element.13, bf16[2048,1024]{1,0:T(8,128)(2,1)} %copy-done.3, s32[]{:T(128)S(6)} %select_n.4, f32[]{:T(128)} %bitcast, bf16[2048,1024]{1,0:T(8,128)(2,1)} %get-tuple-element.10, ...), kind=kOutput, calls=%fused_computation.27 | convolution fusion | flops 538179584 | bytes 5779976 | tf_op jit(solution)/shard_map/dot_general | solution.py:38
  204.0 39.2 %all-reduce = (f32[1024]{0:T(1024)S(1)}, f32[1024]{0:T(1024)S(1)}) all-reduce(f32[1024]{0:T(1024)S(1)} %get-tuple-element.5, f32[1024]{0:T(1024)S(1)} %get-tuple-element.4), channel_id=1, replica_groups=mesh['dp'=16,'feat'=16] {'dp'}, use_global_device_ids=true, to_apply=%region_9.0 | all-reduce | flops 2048 | bytes 16384 | tf_op jit(solution)/shard_map/psum | solution.py:55
  243.2 1.9 fusion.11
  245.2 0.0 all-gather.9.cloned.1.call-update
  246.5 5.3 %copy.7 = f32[1024,1024]{0,1:T(8,128)} copy(f32[1024,1024]{1,0:T(8,128)} %param.8) | data formatting | bytes 8388608 | tf_op args[3]
  251.8 76.1 %psum.31 = f32[]{:T(128)} all-reduce(f32[]{:T(128)S(6)} %add.40), channel_id=1, replica_groups=mesh['dp'=16,'feat'=16] {'dp','feat'}, use_global_device_ids=true, to_apply=%region_12.0 | all-reduce | flops 1 | bytes 8 | tf_op jit(solution)/shard_map/psum | solution.py:53
  328.6 0.0 all-gather.11.cloned.1.call-done
  328.6 0.0 all-gather.9.cloned.1.call-done
  328.6 11.2 %bitcast_add_fusion = f32[1024,1024]{0,1:T(8,128)} fusion(f32[1024,1024]{0,1:T(8,128)} %copy.7, bf16[2048,1024]{1,0:T(8,128)(2,1)} %all-gather.9.cloned.1.call-done, bf16[2048,1024]{1,0:T(8,128)(2,1)} %all-gather.11.cloned.1.call-done), kind=kOutput, calls=%fused_computation.13 | convolution fusion | flops 4296015872 | bytes 16777216 | tf_op jit(solution)/shard_map/dot_general | solution.py:61
  339.8 5.3 %copy.8 = f32[1024,1024]{1,0:T(8,128)} copy(f32[1024,1024]{0,1:T(8,128)} %bitcast_add_fusion) | data formatting | bytes 8388608
  (8 shorter events, 0.0 us)
Async XLA Ops:
  7.2 46.8 %all-gather.7.cloned.1.call-start = ((), (), s32[]{:S(2)}) async-start(), calls=%async_computation.1 | async-start | bytes 4456448 | tf_op jit(solution)/shard_map/all_gather | solution.py:26
  7.9 88.0 %all-gather.5.cloned.1.call-start = ((), (), s32[]{:S(2)}) async-start(), calls=%async_computation | async-start | bytes 4456448 | tf_op jit(solution)/shard_map/all_gather | solution.py:25
  8.6 319.9 %all-gather.11.cloned.1.call-start = ((), (), s32[]{:S(2)}) async-start(), calls=%async_computation.3 | async-start | bytes 4456448 | tf_op jit(solution)/shard_map/all_gather | solution.py:27
  9.4 319.2 %all-gather.9.cloned.1.call-start = ((), (), s32[]{:S(2)}) async-start(), calls=%async_computation.2 | async-start | bytes 4456448 | tf_op jit(solution)/shard_map/all_gather | solution.py:63
  54.0 3.4 copy-start
  95.9 7.1 %copy-start.1 = (bf16[2048,1024]{1,0:T(8,128)(2,1)S(1)}, bf16[2048,1024]{1,0:T(8,128)(2,1)}, u32[]{:S(2)}) copy-start(bf16[2048,1024]{1,0:T(8,128)(2,1)} %all-gather.7.cloned.1.call-done) | copy-start | bytes 12582916
  95.9 7.1 %copy-start.2 = (bf16[2048,1024]{1,0:T(8,128)(2,1)S(1)}, bf16[2048,1024]{1,0:T(8,128)(2,1)}, u32[]{:S(2)}) copy-start(bf16[2048,1024]{1,0:T(8,128)(2,1)} %all-gather.5.cloned.1.call-done) | copy-start | bytes 12582916
  107.0 2.0 copy-start.3
Sparse Core Ops, SparseCore 0:
  9.8 44.0 all-gather.6
  55.8 39.9 all-gather.4
  98.4 116.6 all-gather.10
  245.3 38.2 all-gather.8

commit v2 on v1

v2 whole, which is shorter than its diff:
```python
import functools

import jax
import jax.numpy as jnp
from jax import lax
from jax.experimental import pallas as pl
from jax.experimental.pallas import tpu as pltpu
from jax.sharding import PartitionSpec as P

MESH = pl.DeviceIdType.MESH
BF = jnp.bfloat16
F32 = jnp.float32
off_weight = 0.0051
eps = 1e-05
PEERS = 16
ROWS = 128
COLS = 1024
HALF = ROWS // 2
CHUNK = 32


def remote(src, dst, ss, rs, device):
    return pltpu.make_async_remote_copy(
        src_ref=src, dst_ref=dst, send_sem=ss, recv_sem=rs, device_id=device, device_id_type=MESH
    )


class DpGather:
    def __init__(self, buf, ss, rs, dp):
        self.buf, self.ss, self.rs = buf, ss, rs
        core, y, x = dp % 2, (dp // 2) % 4, dp // 8

        def block(x_, y_):
            return (x_ * 4 + y_) * 2 + core

        low, high, far = (y + 3) % 4, (y + 1) % 4, (y + 2) % 4
        self.own, self.ym, self.yp, self.y2 = (block(x, v) for v in (y, low, high, far))
        self.xo, self.xm, self.xp, self.x2 = (block(1 - x, v) for v in (y, low, high, far))
        self.flip = 1 - 2 * core
        self.table = {
            0: (self.own, None, self.yp, self.ym),
            1: (self.own, None, self.ym, self.yp),
            2: (self.own, None, self.xo, self.xo),
            3: (self.own, None, None, self.own),
            4: (self.ym, 0, self.yp, self.y2),
            5: (self.yp, 1, self.ym, self.y2),
            6: (self.ym, 1, self.xo, self.xm),
            7: (self.yp, 0, self.xo, self.xp),
            8: (self.xo, 0, self.yp, self.xm),
            9: (self.xo, 1, self.ym, self.xp),
            10: (self.ym, None, None, self.ym),
            11: (self.yp, None, None, self.yp),
            12: (self.xo, None, None, self.xo),
            13: (self.y2, None, self.xo, self.x2),
            14: (self.y2, None, None, self.y2),
            15: (self.xm, None, None, self.xm),
            16: (self.xp, None, None, self.xp),
            17: (self.x2, None, None, self.x2),
        }

    def ref(self, block, half):
        if half is None:
            return self.buf.at[block]
        return self.buf.at[block, pl.ds(half * HALF, HALF)]

    def copy(self, slot, received):
        sent, half, target, incoming = self.table[slot]
        if target is None:
            target = self.own + self.flip
            incoming = incoming + self.flip
        ref = self.ref(incoming if received else sent, half)
        return remote(ref, ref, self.ss.at[slot], self.rs.at[slot], {"dp": target})

    def send(self, *slots):
        for slot in slots:
            self.copy(slot, False).start()

    def recv(self, *slots):
        for slot in slots:
            self.copy(slot, True).wait_recv()

    def stage_a(self):
        self.send(0, 1, 2, 3)

    def stage_b(self):
        self.recv(0)
        self.send(4, 6, 10)
        self.recv(1)
        self.send(5, 7, 11)
        self.recv(2)
        self.send(8, 9, 12)

    def stage_c(self):
        self.recv(4, 5)
        self.send(13, 14)
        self.recv(6, 8)
        self.send(15)
        self.recv(7, 9)
        self.send(16)
        self.recv(13)
        self.send(17)

    def drain(self):
        for slot in range(18):
            self.copy(slot, False).wait_send()


class HiddenGather:
    def __init__(self, buf, ss, rs, feat):
        self.buf, self.ss, self.rs = buf, ss, rs
        z, xh = feat // 2, feat % 2
        self.rows = buf.shape[1] // 2

        def at(step, q):
            return ((z + 8 + step) % 8) * 2 + (xh if q == 0 else 1 - xh)

        up, down, partner = at(1, 0), at(-1, 0), at(0, 1)
        self.table = {0: (at(0, 0), None, partner, partner)}
        for q in range(2):
            base = 1 + 8 * q
            for k in range(4):
                last = k == 3
                self.table[base + 2 * k] = (at(-k, q), 0 if last else None, up, at(-k - 1, q))
                self.table[base + 2 * k + 1] = (at(k, q), 1 if last else None, down, at(k + 1, q))

    def copy(self, slot, received):
        sent, half, target, incoming = self.table[slot]
        block = incoming if received else sent
        if half is None:
            ref = self.buf.at[block]
        else:
            ref = self.buf.at[block, pl.ds(half * self.rows, self.rows)]
        return remote(ref, ref, self.ss.at[slot], self.rs.at[slot], {"feat": target})

    def send(self, *slots):
        for slot in slots:
            self.copy(slot, False).start()

    def recv(self, *slots):
        for slot in slots:
            self.copy(slot, True).wait_recv()

    def step(self, q, k):
        base = 1 + 8 * q + 2 * k
        if k:
            self.recv(base - 2, base - 1)
        self.send(base, base + 1)

    def drain(self):
        for slot in range(17):
            self.copy(slot, False).wait_send()


def exchange(axis, me, source, dst, ss, rs):
    def each(act):
        def step(j, carry):
            peer = (me + j) % PEERS
            act(peer)
            return carry

        lax.fori_loop(1, PEERS, step, 0)

    def start():
        each(
            lambda p: remote(source(p), dst.at[me], ss.at[p], rs.at[me], {axis: p}).start()
        )

    def wait_recv():
        each(
            lambda p: remote(source(p), dst.at[p], ss.at[p], rs.at[p], {axis: p}).wait_recv()
        )

    def wait_send():
        each(
            lambda p: remote(source(p), dst.at[me], ss.at[p], rs.at[me], {axis: p}).wait_send()
        )

    return start, wait_recv, wait_send


def over_rows(step, init):
    per = ROWS // CHUNK

    def body(i, carry):
        return step(i // per, pl.ds(pl.multiple_of((i % per) * CHUNK, CHUNK), CHUNK), carry)

    return lax.fori_loop(0, PEERS * per, body, init)


def fold(values):
    return jnp.sum(values.reshape(CHUNK // 8, 8, COLS), axis=0)


def statistics(buf, batch):
    zero = jnp.zeros((8, COLS), F32)

    def add(block, rows, acc):
        return acc + fold(buf[block, rows].astype(F32))

    centre = jnp.sum(over_rows(add, zero), axis=0, keepdims=True) / batch

    def add_square(block, rows, acc):
        off = buf[block, rows].astype(F32) - centre
        return acc + fold(off * off)

    spread = jnp.sum(over_rows(add_square, zero), axis=0, keepdims=True) / batch
    return centre, lax.rsqrt(spread + eps)


def kernel(
    z_one, z_two, hidden, scale_ref,
    weight, loss_ref,
    one, two, grad, hid, raw, part, part_in, gram, spread, sums, losses,
    local_sem, one_s, one_r, two_s, two_r, grad_s, grad_r, hid_s, hid_r,
    part_s, part_r, gram_s, gram_r, sums_s, sums_r, loss_s, loss_r,
):
    dp, feat = lax.axis_index("dp"), lax.axis_index("feat")
    batch = ROWS * PEERS
    width = COLS * PEERS

    local = [
        pltpu.make_async_copy(z_two, two.at[dp], local_sem.at[0]),
        pltpu.make_async_copy(z_one, one.at[dp], local_sem.at[1]),
        pltpu.make_async_copy(hidden, raw, local_sem.at[2]),
    ]
    for copy in local:
        copy.start()

    barrier = pltpu.get_barrier_semaphore()

    def greet(j, carry):
        pl.semaphore_signal(
            barrier, inc=1, device_id={"dp": (dp + j) % PEERS}, device_id_type=MESH
        )
        pl.semaphore_signal(
            barrier, inc=1, device_id={"feat": (feat + j) % PEERS}, device_id_type=MESH
        )
        return carry

    lax.fori_loop(1, PEERS, greet, 0)
    for copy in local:
        copy.wait()
    pl.semaphore_wait(barrier, 2 * (PEERS - 1))

    gather_two = DpGather(two, two_s, two_r, dp)
    gather_one = DpGather(one, one_s, one_r, dp)
    gather_grad = DpGather(grad, grad_s, grad_r, dp)
    gather_hid = HiddenGather(hid, hid_s, hid_r, feat)

    gather_two.stage_a()
    hid[feat] = raw[...].T
    gather_hid.send(0)
    gather_hid.step(0, 0)
    gather_two.stage_b()
    gather_one.stage_a()
    gather_hid.recv(0)
    gather_hid.step(1, 0)
    gather_two.stage_c()
    gather_hid.step(0, 1)
    gather_two.recv(3, 10, 11, 12, 14, 15, 16, 17)
    gather_two.drain()

    centre, inverse = statistics(two, batch)

    def norm_two(block, rows, carry):
        two[block, rows] = ((two[block, rows].astype(F32) - centre) * inverse).astype(BF)
        return carry

    over_rows(norm_two, 0)

    def gram_tiles(j, carry):
        pair = two[pl.ds(2 * j, 2)].reshape(2 * ROWS, COLS)
        tile = lax.dot_general(
            two[dp], pair, (((1,), (1,)), ((), ())), preferred_element_type=F32
        ).astype(BF)
        part[2 * j] = tile[:, :ROWS]
        part[2 * j + 1] = tile[:, ROWS:]
        return carry

    lax.fori_loop(0, PEERS // 2, gram_tiles, 0)
    part_start, part_recv, part_send = exchange(
        "feat", feat, lambda p: part.at[p], part_in, part_s, part_r
    )
    part_start()
    gather_one.stage_b()
    gather_hid.step(1, 1)
    part_in[feat] = part[feat]
    part_recv()

    def add_part(j, acc):
        return acc + part_in[j].astype(F32)

    gram[feat] = lax.fori_loop(0, PEERS, add_part, jnp.zeros((ROWS, ROWS), F32)).astype(BF)
    gram_start, gram_recv, gram_send = exchange(
        "feat", feat, lambda p: gram.at[feat], gram, gram_s, gram_r
    )
    gram_start()
    gather_one.stage_c()
    gather_one.recv(3, 10, 11, 12, 14, 15, 16, 17)
    gather_one.drain()

    centre_one, inverse_one = statistics(one, batch)

    def norm_one(block, rows, acc):
        normed = ((one[block, rows].astype(F32) - centre_one) * inverse_one).astype(BF)
        one[block, rows] = normed
        return acc + fold(normed.astype(F32) * two[block, rows].astype(F32))

    corr = (
        jnp.sum(over_rows(norm_one, jnp.zeros((8, COLS), F32)), axis=0, keepdims=True) / batch
    )
    scale = scale_ref[0] / batch
    weight_diag = scale * (-2.0 * (1.0 - corr) - 2.0 * off_weight * corr)

    gather_hid.step(0, 2)
    gram_recv()
    gather_hid.step(1, 2)

    spread[...] = jnp.zeros_like(spread)

    def spread_step(j, carry):
        rows = jnp.concatenate([gram[2 * j], gram[2 * j + 1]], axis=1)
        spread[...] += jnp.dot(
            rows, one[pl.ds(2 * j, 2)].reshape(2 * ROWS, COLS), preferred_element_type=F32
        )
        return carry

    lax.fori_loop(0, PEERS // 2, spread_step, 0)
    factor = scale * (2.0 * off_weight / batch)
    zero = jnp.zeros((8, COLS), F32)

    def norm_step(i, accs):
        rows = pl.ds(pl.multiple_of(i * CHUNK, CHUNK), CHUNK)
        raw_spread = spread[rows]
        share = one[dp, rows].astype(F32)
        value = raw_spread * factor + two[dp, rows].astype(F32) * weight_diag
        spread[rows] = value
        return (
            accs[0] + fold(value),
            accs[1] + fold(value * share),
            accs[2] + fold(raw_spread * share),
        )

    accs = lax.fori_loop(0, ROWS // CHUNK, norm_step, (zero, zero, zero))
    square = jnp.sum(accs[2], axis=0, keepdims=True) / (float(batch) * float(batch))
    terms = off_weight * square + (
        (1.0 - corr) * (1.0 - corr) - off_weight * corr * corr
    ) * (1.0 / PEERS)
    lanes = terms[:, :128]
    for k in range(1, COLS // 128):
        lanes = lanes + terms[:, k * 128 : (k + 1) * 128]
    sums[dp, 0:1, :COLS] = jnp.sum(accs[0], axis=0, keepdims=True)
    sums[dp, 1:2, :COLS] = jnp.sum(accs[1], axis=0, keepdims=True)
    sums[dp, 0:1, COLS:] = lanes
    sums[dp, 1:2, COLS:] = jnp.zeros_like(lanes)
    sums_start, sums_recv, sums_send = exchange(
        "dp", dp, lambda p: sums.at[dp], sums, sums_s, sums_r
    )
    sums_start()
    sums_recv()

    total = lax.fori_loop(
        0, PEERS, lambda j, acc: acc + sums[j], jnp.zeros((2, COLS + 128), F32)
    )
    mean_grad = total[0:1, :COLS] / batch
    mean_cross = total[1:2, :COLS] / batch

    def grad_step(i, carry):
        rows = pl.ds(pl.multiple_of(i * CHUNK, CHUNK), CHUNK)
        share = one[dp, rows].astype(F32)
        grad[dp, rows] = ((spread[rows] - mean_grad - share * mean_cross) * inverse_one).astype(BF)
        return carry

    lax.fori_loop(0, ROWS // CHUNK, grad_step, 0)
    gather_grad.stage_a()
    losses[feat] = total[:, COLS:]
    loss_start, loss_recv, loss_send = exchange(
        "feat", feat, lambda p: losses.at[feat], losses, loss_s, loss_r
    )
    loss_start()
    gather_hid.step(0, 3)
    gather_hid.step(1, 3)
    weight[...] = jnp.zeros_like(weight)
    gather_grad.stage_b()
    gather_hid.recv(7, 8, 15, 16)

    def add_pair(block):
        pair = block // 2
        rhs = grad[pl.ds(2 * pair, 2)].reshape(2 * ROWS, COLS)

        def step(i, carry):
            rows = pl.ds(pl.multiple_of(i * 256, 256), 256)
            lhs = jnp.concatenate([hid[2 * pair, rows], hid[2 * pair + 1, rows]], axis=1)
            weight[rows] += jnp.dot(lhs, rhs, preferred_element_type=F32)
            return carry

        lax.fori_loop(0, COLS // 256, step, 0)

    gather_grad.recv(3)
    add_pair(gather_grad.own)
    gather_grad.recv(10)
    add_pair(gather_grad.ym)
    gather_grad.stage_c()
    gather_grad.recv(11)
    add_pair(gather_grad.yp)
    gather_grad.recv(12)
    add_pair(gather_grad.xo)
    gather_grad.recv(14)
    add_pair(gather_grad.y2)
    gather_grad.recv(15)
    add_pair(gather_grad.xm)
    gather_grad.recv(16)
    add_pair(gather_grad.xp)
    gather_grad.recv(17)
    add_pair(gather_grad.x2)

    loss_recv()
    all_loss = lax.fori_loop(
        0, PEERS, lambda j, acc: acc + losses[j], jnp.zeros((2, 128), F32)
    )
    loss_ref[...] = jnp.broadcast_to(
        jnp.sum(all_loss, axis=(0, 1), keepdims=True) / width, loss_ref.shape
    )
    part_send()
    gram_send()
    sums_send()
    loss_send()
    gather_grad.drain()
    gather_hid.drain()


def body(z_one, z_two, hidden_in, grad_acc, loss_scale):
    any_space = pl.BlockSpec(memory_space=pl.ANY)
    dma = pltpu.SemaphoreType.DMA
    weight_grad, loss = pl.pallas_call(
        kernel,
        out_shape=(
            jax.ShapeDtypeStruct((COLS, COLS), F32),
            jax.ShapeDtypeStruct((8, 128), F32),
        ),
        in_specs=[any_space] * 3 + [pl.BlockSpec(memory_space=pltpu.SMEM)],
        out_specs=(
            pl.BlockSpec(memory_space=pltpu.VMEM),
            pl.BlockSpec(memory_space=pltpu.VMEM),
        ),
        scratch_shapes=[
            pltpu.VMEM((PEERS, ROWS, COLS), BF),
            pltpu.VMEM((PEERS, ROWS, COLS), BF),
            pltpu.VMEM((PEERS, ROWS, COLS), BF),
            pltpu.VMEM((PEERS, COLS, ROWS), BF),
            pltpu.VMEM((ROWS, COLS), BF),
            pltpu.VMEM((PEERS, ROWS, ROWS), BF),
            pltpu.VMEM((PEERS, ROWS, ROWS), BF),
            pltpu.VMEM((PEERS, ROWS, ROWS), BF),
            pltpu.VMEM((ROWS, COLS), F32),
            pltpu.VMEM((PEERS, 2, COLS + 128), F32),
            pltpu.VMEM((PEERS, 2, 128), F32),
            dma((3,)),
        ]
        + [dma((18,))] * 6
        + [dma((17,))] * 2
        + [dma((PEERS,))] * 8,
        compiler_params=pltpu.CompilerParams(
            collective_id=0, has_side_effects=True, vmem_limit_bytes=48 << 20
        ),
        cost_estimate=pl.CostEstimate(
            flops=6 * 10**9, bytes_accessed=8 * 10**6, transcendentals=0
        ),
        name="barlow",
    )(z_one, z_two, hidden_in, loss_scale)
    return grad_acc + weight_grad, loss[0, :1]


def solution(mesh):
    placed = (P("dp", "feat"), P("dp", "feat"), P("feat", "dp"), P("dp", "feat"), P())
    return jax.shard_map(
        body, mesh=mesh, in_specs=placed, out_specs=(P("dp", "feat"), P()), check_vma=False
    )
```

time: 353 us -> 132 us (0.37)
  blocking collectives: 204 us -> 0 us
  Pallas kernels: 0 us -> 122 us
  waiting for transfers between devices: 83.3 us -> 0 us
  matrix products: 16.6 us -> 0 us
  between operations: 17.5 us -> 1.3 us
  other arithmetic: 17.8 us -> 2.98 us
  local copies, waits for them, and re-layouts: 13.1 us -> 3.36 us
    psum x3 -> x0, blocking collectives: 204 us -> none  [the longest x1 89.1 us: body(): lax.psum(lax.dot_general(own_two, normed_two, (((1,), (1,)), ((), ())), p...]
    pallas_call x0 -> x1, Pallas kernels: none -> 122 us  [body(): pl.pallas_call(kernel, out_shape=(jax.ShapeDtypeStruct((COLS, COLS), F32)...]
    all_gather x4 -> x0, waiting for transfers between devices: 81.2 us -> none  [the longest x1 43.9 us: body(): one_all = lax.all_gather(z_one, 'dp', axis=0, tiled=True)]
    dot_general x3 -> x0, matrix products: 16.6 us -> none  [the longest x1 11.2 us: body(): lax.dot_general(hidden_all, lax.all_gather(grad_z, 'dp', axis=0, tiled=Tr...]
    reduce_sum x6 -> x0, other arithmetic: 15.9 us -> none  [the longest x2 6.07 us: standardize(): centre = jnp.mean(values, axis=0)]
    unnamed x10 -> x8, local copies, waits for them, and re-layouts: 13.1 us -> 2.85 us
  transfers between devices with their start and end apart: 4 -> 0, of which waited for: 2 -> 0; matrix products, arithmetic and copies ran while one was open for 8% -> 0% of each run, Pallas kernels for 0% -> 0%
where the time goes in v2:
time: 132 us; the launch traced here: 130 us
  Pallas kernels  122 us (92%)
  local copies, waits for them, and re-layouts  3.36 us (3%)
  other arithmetic  2.98 us (2%)
    pallas_call x1, Pallas kernels, body(): pl.pallas_call(kernel, out_shape=(jax.ShapeDtypeStruct((COLS, COLS), F32)...  122 us
    add x1, other arithmetic, body(): return (grad_acc + weight_grad, loss[0, :1])  2.98 us
    unnamed x8, local copies, waits for them, and re-layouts  2.85 us

profile of v2, /device:TPU:1, one launch (start us, length us, event | category | flops | bytes accessed | tf_op | source)
XLA Modules:
  0.0 130.1 jit_solution(11967331303718372530)
XLA Ops:
  1.3 0.0 copy-start
  1.3 0.9 copy-done
  2.2 0.0 copy-start.1
  2.2 0.9 copy-done.1
  3.2 0.0 copy-start.2
  3.2 0.9 copy-done.2
  4.1 0.0 copy-start.3
  4.1 122.5 %barlow.1 = (f32[1024,1024]{1,0:T(8,128)S(1)}, f32[8,128]{1,0:T(8,128)S(1)}) custom-call(bf16[128,1024]{1,0:T(8,128)(2,1)S(1)} %copy-done, bf16[128,1024]{1,0:T(8,128)(2,1)S(1)} %copy-done.1, bf16[128,1024]{1,0:T(8,128)(2,1)S(1)} %copy-done.2, f32[1]{0:T(128)S(6)} %copy.7.scale_ref), custom_call_target="tpu_custom_call" | custom-call | flops 6000000000 | bytes 8000000 | tf_op jit(solution)/shard_map/barlow/pallas_call | solution.py:435
  126.6 0.5 slice.3
  127.1 0.0 copy-done.3
  127.1 3.0 %add.3 = f32[1024,1024]{1,0:T(8,128)} add(f32[1024,1024]{1,0:T(8,128)S(1)} %copy-done.3, f32[1024,1024]{1,0:T(8,128)S(1)} %get-tuple-element.4) | non-fusion elementwise | flops 1048576 | bytes 12582912 | tf_op jit(solution)/shard_map/add | solution.py:471
Async XLA Ops:
  1.3 1.0 copy-start
  2.2 0.9 copy-start.1
  3.2 0.9 copy-start.2
  4.1 123.0 %copy-start.3 = (f32[1024,1024]{1,0:T(8,128)S(1)}, f32[1024,1024]{1,0:T(8,128)}, u32[]{:S(2)}) copy-start(f32[1024,1024]{1,0:T(8,128)} %param.8) | copy-start | bytes 12582916

commit v3 on v2

v3 whole, which is shorter than its diff:
```python
import jax
import jax.numpy as jnp
from jax import lax
from jax.experimental import pallas as pl
from jax.experimental.pallas import tpu as pltpu
from jax.sharding import PartitionSpec as P

MESH = pl.DeviceIdType.MESH
BF = jnp.bfloat16
F32 = jnp.float32
off_weight = 0.0051
eps = 1e-05
PEERS = 16
ROWS = 128
COLS = 1024
HALF = ROWS // 2
CHUNK = 64


def remote(src, dst, ss, rs, device):
    return pltpu.make_async_remote_copy(
        src_ref=src, dst_ref=dst, send_sem=ss, recv_sem=rs, device_id=device, device_id_type=MESH
    )


class DpGather:
    def __init__(self, buf, ss, rs, dp):
        self.buf, self.ss, self.rs = buf, ss, rs
        core, y, x = dp % 2, (dp // 2) % 4, dp // 8

        def block(x_, y_):
            return (x_ * 4 + y_) * 2 + core

        low, high, far = (y + 3) % 4, (y + 1) % 4, (y + 2) % 4
        self.own, self.ym, self.yp, self.y2 = (block(x, v) for v in (y, low, high, far))
        self.xo, self.xm, self.xp, self.x2 = (block(1 - x, v) for v in (y, low, high, far))
        self.flip = 1 - 2 * core
        self.any_peer = {"dp": self.xo}
        self.table = [
            (self.own, 0, self.yp, self.ym),
            (self.own, 1, self.yp, self.ym),
            (self.own, 1, self.ym, self.yp),
            (self.own, 0, self.ym, self.yp),
            (self.own, None, self.xo, self.xo),
            (self.own, None, None, self.own),
            (self.ym, 0, self.yp, self.y2),
            (self.yp, 1, self.ym, self.y2),
            (self.xo, None, self.yp, self.xm),
            (self.xo, None, self.ym, self.xp),
            (self.y2, 0, self.xo, self.x2),
            (self.y2, 1, self.xo, self.x2),
            (self.ym, None, None, self.ym),
            (self.yp, None, None, self.yp),
            (self.xo, None, None, self.xo),
            (self.y2, None, None, self.y2),
            (self.xm, None, None, self.xm),
            (self.xp, None, None, self.xp),
            (self.x2, None, None, self.x2),
        ]
        self.near = [(v // 2, slot) for v, slot in ((self.own, 5), (self.xo, 14), (self.ym, 12), (self.yp, 13))]
        self.later = [(v // 2, slot) for v, slot in ((self.y2, 15), (self.xm, 16), (self.xp, 17), (self.x2, 18))]

    def copy(self, slot, received):
        sent, half, target, incoming = self.table[slot]
        if target is None:
            target = self.own + self.flip
            incoming = incoming + self.flip
        block = incoming if received else sent
        ref = self.buf.at[block]
        if half is not None:
            ref = self.buf.at[block, pl.ds(half * HALF, HALF)]
        return remote(ref, ref, self.ss, self.rs.at[slot], {"dp": target})

    def send(self, *slots):
        for slot in slots:
            self.copy(slot, False).start()

    def recv(self, *slots):
        for slot in slots:
            self.copy(slot, True).wait_recv()

    def stage_a(self):
        self.send(0, 2, 1, 3, 4, 5)

    def stage_b(self):
        self.recv(0)
        self.send(6)
        self.recv(2)
        self.send(7)
        self.recv(4)
        self.send(8, 9, 14)
        self.recv(1)
        self.send(12)
        self.recv(3)
        self.send(13)

    def stage_c(self):
        self.recv(6)
        self.send(10)
        self.recv(7)
        self.send(11, 15)

    def stage_d(self):
        self.recv(8)
        self.send(16)
        self.recv(9)
        self.send(17)
        self.recv(10, 11)
        self.send(18)

    def drain(self):
        every = self.buf.at[pl.ds(0, PEERS - 1)]
        remote(every, every, self.ss, self.rs.at[0], self.any_peer).wait_send()


class HiddenGather:
    def __init__(self, buf, ss, rs, feat):
        self.buf, self.ss, self.rs = buf, ss, rs
        z, xh = feat // 2, feat % 2
        self.rows = buf.shape[1] // 2

        def at(step, q):
            return ((z + 8 + step) % 8) * 2 + (xh if q == 0 else 1 - xh)

        up, down, partner = at(1, 0), at(-1, 0), at(0, 1)
        self.any_peer = {"feat": partner}
        self.table = {0: (at(0, 0), None, partner, partner)}
        for q in range(2):
            base = 1 + 8 * q
            for k in range(4):
                last = k == 3
                self.table[base + 2 * k] = (at(-k, q), 0 if last else None, up, at(-k - 1, q))
                self.table[base + 2 * k + 1] = (at(k, q), 1 if last else None, down, at(k + 1, q))

    def copy(self, slot, received):
        sent, half, target, incoming = self.table[slot]
        block = incoming if received else sent
        if half is None:
            ref = self.buf.at[block]
        else:
            ref = self.buf.at[block, pl.ds(half * self.rows, self.rows)]
        return remote(ref, ref, self.ss, self.rs.at[slot], {"feat": target})

    def send(self, *slots):
        for slot in slots:
            self.copy(slot, False).start()

    def recv(self, *slots):
        for slot in slots:
            self.copy(slot, True).wait_recv()

    def step(self, q, k):
        base = 1 + 8 * q + 2 * k
        if k:
            self.recv(base - 2, base - 1)
        self.send(base, base + 1)

    def drain(self):
        every = self.buf.at[pl.ds(0, PEERS - 1)]
        remote(every, every, self.ss, self.rs.at[0], self.any_peer).wait_send()


def exchange(axis, me, source, dst, ss, rs):
    others = dst.at[pl.ds(0, PEERS - 1)]

    def start():
        def step(j, carry):
            peer = (me + j) % PEERS
            remote(source(peer), dst.at[me], ss, rs, {axis: peer}).start()
            return carry

        lax.fori_loop(1, PEERS, step, 0)

    def all_of_them():
        return remote(others, others, ss, rs, {axis: (me + 1) % PEERS})

    return start, lambda: all_of_them().wait_recv(), lambda: all_of_them().wait_send()


def fold(values):
    return jnp.sum(values.reshape(CHUNK // 8, 8, COLS), axis=0)


def over_rows(blocks, step, init):
    per = ROWS // CHUNK

    def body(i, carry):
        return step(i // per, pl.ds(pl.multiple_of((i % per) * CHUNK, CHUNK), CHUNK), carry)

    return lax.fori_loop(0, blocks * per, body, init)


def local_statistics(ref):
    zero = jnp.zeros((8, COLS), F32)

    def add(block, rows, acc):
        return acc + fold(ref[rows].astype(F32))

    mean = jnp.sum(over_rows(1, add, zero), axis=0, keepdims=True) / ROWS

    def add_square(block, rows, acc):
        off = ref[rows].astype(F32) - mean
        return acc + fold(off * off)

    return mean, jnp.sum(over_rows(1, add_square, zero), axis=0, keepdims=True)


def merge_statistics(stats, view, batch):
    zero = jnp.zeros((1, COLS), F32)
    centre = lax.fori_loop(
        0, PEERS, lambda j, acc: acc + stats[view, j, 0:1], zero
    ) / PEERS

    def add(j, acc):
        off = stats[view, j, 0:1] - centre
        return acc + (stats[view, j, 1:2] + off * off * ROWS)

    spread = lax.fori_loop(0, PEERS, add, zero) / batch
    return centre, lax.rsqrt(spread + eps)


def kernel(
    packed, scale_ref,
    weight, loss_ref,
    one, two, grad, hid, normed_one, normed_two, fixed, raw, part, part_in, gram, spread, stats, sums, losses,
    local_sem, one_s, one_r, two_s, two_r, grad_s, grad_r, hid_s, hid_r,
    part_s, part_r, gram_s, gram_r, stats_s, stats_r, sums_s, sums_r, loss_s, loss_r,
):
    dp, feat = lax.axis_index("dp"), lax.axis_index("feat")
    batch = ROWS * PEERS
    width = COLS * PEERS

    local = [
        pltpu.make_async_copy(packed.at[0], two.at[dp], local_sem.at[0]),
        pltpu.make_async_copy(packed.at[1], one.at[dp], local_sem.at[1]),
        pltpu.make_async_copy(packed.at[2], raw, local_sem.at[2]),
    ]
    for copy in local:
        copy.start()

    barrier = pltpu.get_barrier_semaphore()

    def greet(j, carry):
        pl.semaphore_signal(
            barrier, inc=1, device_id={"dp": (dp + j) % PEERS}, device_id_type=MESH
        )
        pl.semaphore_signal(
            barrier, inc=1, device_id={"feat": (feat + j) % PEERS}, device_id_type=MESH
        )
        return carry

    lax.fori_loop(1, PEERS, greet, 0)
    for copy in local:
        copy.wait()

    gather_two = DpGather(two, two_s, two_r, dp)
    gather_one = DpGather(one, one_s, one_r, dp)
    gather_grad = DpGather(grad, grad_s, grad_r, dp)
    gather_hid = HiddenGather(hid, hid_s, hid_r, feat)
    stats_moves = [
        exchange("dp", dp, source(k), stats.at[k], stats_s.at[k], stats_r.at[k])
        for source, k in ((lambda k: lambda p: stats.at[k, dp], v) for v in range(2))
    ]
    part_moves, gram_moves = [
        [exchange("feat", feat, source(k), dst.at[k], ss.at[k], rs.at[k]) for k in range(2)]
        for source, dst, ss, rs in (
            (lambda k: lambda p: part.at[k, p], part_in, part_s, part_r),
            (lambda k: lambda p: gram.at[k, feat], gram, gram_s, gram_r),
        )
    ]
    pl.semaphore_wait(barrier, 2 * (PEERS - 1))

    gather_two.stage_a()

    def start_statistics(view, buf):
        mean, square = local_statistics(buf.at[dp])
        stats[view, dp, 0:1] = mean
        stats[view, dp, 1:2] = square
        stats_moves[view][0]()

    start_statistics(0, two)
    hid[feat] = raw[...].T
    gather_hid.send(0)
    gather_hid.step(0, 0)
    gather_two.stage_b()
    stats_moves[0][1]()
    centre, inverse = merge_statistics(stats, 0, batch)

    def gram_pair(group, place, pair):
        def norm(block, rows, carry):
            values = two[2 * pair + block, rows].astype(F32)
            normed_two[2 * pair + block, rows] = ((values - centre) * inverse).astype(BF)
            return carry

        over_rows(2, norm, 0)
        tile = lax.dot_general(
            normed_two[dp],
            normed_two[pl.ds(2 * pair, 2)].reshape(2 * ROWS, COLS),
            (((1,), (1,)), ((), ())),
            preferred_element_type=F32,
        ).astype(BF)
        first = 4 * place
        part[group, first : first + 2] = tile[:, :ROWS].reshape(2, HALF, ROWS)
        part[group, first + 2 : first + 4] = tile[:, ROWS:].reshape(2, HALF, ROWS)

    def add_parts(group):
        part_in[group, feat] = part[group, feat]
        part_moves[group][1]()

        def add(j, acc):
            return acc + part_in[group, j].astype(F32)

        gram[group, feat] = lax.fori_loop(0, PEERS, add, jnp.zeros((HALF, ROWS), F32)).astype(BF)
        gram_moves[group][0]()

    for place, (pair, slot) in enumerate(gather_two.near):
        gather_two.recv(slot)
        gram_pair(0, place, pair)
    part_moves[0][0]()
    gather_hid.recv(0)
    gather_hid.step(1, 0)
    gather_two.stage_c()
    gather_two.recv(15)
    gram_pair(1, 0, gather_two.later[0][0])
    gather_hid.step(0, 1)
    add_parts(0)
    gather_two.stage_d()
    gather_one.stage_a()
    start_statistics(1, one)
    for place, (pair, slot) in list(enumerate(gather_two.later))[1:]:
        gather_two.recv(slot)
        gram_pair(1, place, pair)
    part_moves[1][0]()
    gather_hid.step(1, 1)
    gather_one.stage_b()
    add_parts(1)
    gather_hid.step(0, 2)

    stats_moves[1][1]()
    centre_one, inverse_one = merge_statistics(stats, 1, batch)

    def norm_pair(pair, acc):
        def norm(block, rows, acc):
            values = one[2 * pair + block, rows].astype(F32)
            normed = ((values - centre_one) * inverse_one).astype(BF)
            normed_one[2 * pair + block, rows] = normed
            return acc + fold(
                normed.astype(F32) * normed_two[2 * pair + block, rows].astype(F32)
            )

        return over_rows(2, norm, acc)

    acc = jnp.zeros((8, COLS), F32)
    for pair, slot in gather_one.near:
        gather_one.recv(slot)
        acc = norm_pair(pair, acc)
    gather_one.stage_c()
    gather_hid.step(1, 2)
    gather_one.stage_d()
    for pair, slot in gather_one.later:
        gather_one.recv(slot)
        acc = norm_pair(pair, acc)
    corr = jnp.sum(acc, axis=0, keepdims=True) / batch
    scale = scale_ref[0] / batch
    weight_diag = scale * (-2.0 * (1.0 - corr) - 2.0 * off_weight * corr)

    def add_spread(group, pairs):
        for place, (pair, _) in enumerate(pairs):
            first = 4 * place
            rows = jnp.concatenate(
                [
                    gram[group, first : first + 2].reshape(ROWS, ROWS),
                    gram[group, first + 2 : first + 4].reshape(ROWS, ROWS),
                ],
                axis=1,
            )
            product = jnp.dot(
                rows,
                normed_one[pl.ds(2 * pair, 2)].reshape(2 * ROWS, COLS),
                preferred_element_type=F32,
            )
            if group == 0 and place == 0:
                spread[...] = product
            else:
                spread[...] += product

    gram_moves[0][1]()
    add_spread(0, gather_one.near)
    gram_moves[1][1]()
    add_spread(1, gather_one.later)
    factor = scale * (2.0 * off_weight / batch)
    zero = jnp.zeros((8, COLS), F32)

    def norm_step(block, rows, accs):
        raw_spread = spread[rows]
        share = normed_one[dp, rows].astype(F32)
        value = raw_spread * factor + normed_two[dp, rows].astype(F32) * weight_diag
        spread[rows] = value
        return (
            accs[0] + fold(value),
            accs[1] + fold(value * share),
            accs[2] + fold(raw_spread * share),
        )

    accs = over_rows(1, norm_step, (zero, zero, zero))
    sum_grad = jnp.sum(accs[0], axis=0, keepdims=True)
    sum_cross = jnp.sum(accs[1], axis=0, keepdims=True)
    near_grad = sum_grad / ROWS
    near_cross = sum_cross / ROWS

    def grad_step(block, rows, carry):
        share = normed_one[dp, rows].astype(F32)
        grad[dp, rows] = (spread[rows] - near_grad - share * near_cross).astype(BF)
        return carry

    over_rows(1, grad_step, 0)
    gather_grad.stage_a()
    square = jnp.sum(accs[2], axis=0, keepdims=True) / (float(batch) * float(batch))
    terms = off_weight * square + (
        (1.0 - corr) * (1.0 - corr) - off_weight * corr * corr
    ) * (1.0 / PEERS)
    lanes = terms[:, :128]
    for k in range(1, COLS // 128):
        lanes = lanes + terms[:, k * 128 : (k + 1) * 128]
    sums[dp, 0:1, :COLS] = sum_grad
    sums[dp, 1:2, :COLS] = sum_cross
    sums[dp, 0:1, COLS:] = lanes
    sums[dp, 1:2, COLS:] = jnp.zeros_like(lanes)
    sums_start, sums_recv, sums_send = exchange(
        "dp", dp, lambda p: sums.at[dp], sums, sums_s, sums_r
    )
    sums_start()
    gather_hid.step(0, 3)
    gather_grad.stage_b()
    sums_recv()
    total = lax.fori_loop(
        0, PEERS, lambda j, acc: acc + sums[j], jnp.zeros((2, COLS + 128), F32)
    )
    losses[feat] = total[:, COLS:]
    loss_start, loss_recv, loss_send = exchange(
        "feat", feat, lambda p: losses.at[feat], losses, loss_s, loss_r
    )
    loss_start()
    gather_hid.step(1, 3)
    mean_grad = total[0:1, :COLS] / batch
    mean_cross = total[1:2, :COLS] / batch

    def fix_pair(pair, place):
        for block in range(2):
            at = 2 * pair + block
            shift = mean_grad - sums[at, 0:1, :COLS] / ROWS
            tilt = mean_cross - sums[at, 1:2, :COLS] / ROWS

            def fix(i, rows, carry):
                share = normed_one[at, rows].astype(F32)
                value = grad[at, rows].astype(F32) - shift - share * tilt
                fixed[2 * place + block, rows] = (value * inverse_one).astype(BF)
                return carry

            over_rows(1, fix, 0)

    def add_pairs(pairs, first):
        count = 2 * len(pairs)

        def step(i, carry):
            rows = pl.ds(pl.multiple_of(i * 512, 512), 512)
            lhs = jnp.concatenate(
                [hid[2 * pair + block, rows] for pair in pairs for block in range(2)], axis=1
            )
            product = jnp.dot(
                lhs, fixed[:count].reshape(count * ROWS, COLS), preferred_element_type=F32
            )
            if first:
                weight[rows] = product
            else:
                weight[rows] += product
            return carry

        lax.fori_loop(0, COLS // 512, step, 0)

    def finish_pairs(group, first):
        for place, (pair, slot) in enumerate(group):
            gather_grad.recv(slot)
            fix_pair(pair, place)
        add_pairs([pair for pair, _ in group], first)

    gather_hid.recv(7, 8, 15, 16)
    finish_pairs(gather_grad.near[:2], True)
    gather_grad.stage_c()
    finish_pairs(gather_grad.near[2:], False)
    gather_grad.stage_d()
    finish_pairs(gather_grad.later[:1], False)
    finish_pairs(gather_grad.later[1:], False)

    loss_recv()
    all_loss = lax.fori_loop(
        0, PEERS, lambda j, acc: acc + losses[j], jnp.zeros((2, 128), F32)
    )
    loss_ref[0] = jnp.sum(all_loss) / width
    gather_two.drain()
    gather_one.drain()
    gather_grad.drain()
    gather_hid.drain()
    for group in range(2):
        stats_moves[group][2]()
        part_moves[group][2]()
        gram_moves[group][2]()
    sums_send()
    loss_send()


def body(z_one, z_two, hidden_in, grad_acc, loss_scale):
    in_hbm = pl.BlockSpec(memory_space=pltpu.HBM)
    in_smem = pl.BlockSpec(memory_space=pltpu.SMEM)
    dma = pltpu.SemaphoreType.DMA
    weight_grad, loss = pl.pallas_call(
        kernel,
        out_shape=(
            jax.ShapeDtypeStruct((COLS, COLS), F32),
            jax.ShapeDtypeStruct((1,), F32),
        ),
        in_specs=[in_hbm, in_smem],
        out_specs=(pl.BlockSpec(memory_space=pltpu.VMEM), in_smem),
        scratch_shapes=[
            pltpu.VMEM((PEERS, ROWS, COLS), BF),
            pltpu.VMEM((PEERS, ROWS, COLS), BF),
            pltpu.VMEM((PEERS, ROWS, COLS), BF),
            pltpu.VMEM((PEERS, COLS, ROWS), BF),
            pltpu.VMEM((PEERS, ROWS, COLS), BF),
            pltpu.VMEM((PEERS, ROWS, COLS), BF),
            pltpu.VMEM((6, ROWS, COLS), BF),
            pltpu.VMEM((ROWS, COLS), BF),
            pltpu.VMEM((2, PEERS, HALF, ROWS), BF),
            pltpu.VMEM((2, PEERS, HALF, ROWS), BF),
            pltpu.VMEM((2, PEERS, HALF, ROWS), BF),
            pltpu.VMEM((ROWS, COLS), F32),
            pltpu.VMEM((2, PEERS, 2, COLS), F32),
            pltpu.VMEM((PEERS, 2, COLS + 128), F32),
            pltpu.VMEM((PEERS, 2, 128), F32),
            dma((3,)),
        ]
        + [dma, dma((19,))] * 3
        + [dma, dma((17,))]
        + [dma((2,))] * 6
        + [dma] * 4,
        compiler_params=pltpu.CompilerParams(
            collective_id=0, has_side_effects=True, vmem_limit_bytes=48 << 20
        ),
        cost_estimate=pl.CostEstimate(
            flops=6 * 10**9, bytes_accessed=8 * 10**6, transcendentals=0
        ),
        name="barlow",
    )(jnp.stack([z_two, z_one, hidden_in]), loss_scale)
    return grad_acc + weight_grad, loss


def solution(mesh):
    placed = (P("dp", "feat"), P("dp", "feat"), P("feat", "dp"), P("dp", "feat"), P())
    return jax.shard_map(
        body, mesh=mesh, in_specs=placed, out_specs=(P("dp", "feat"), P()), check_vma=False
    )
```

time: 132 us -> 108 us (0.82); the launches traced: 130 us -> 108 us
  Pallas kernels: 122 us -> 100 us
  local copies, waits for them, and re-layouts: 3.36 us -> 0.01 us
  between operations: 1.3 us -> 3.07 us
    pallas_call x1, Pallas kernels: 122 us -> 100 us  [body(): pl.pallas_call(kernel, out_shape=(jax.ShapeDtypeStruct((COLS, COLS), F32)...]
    unnamed x8 -> x2, local copies, waits for them, and re-layouts: 2.85 us -> 0.01 us
where the time goes in v3:
time: 108 us
  Pallas kernels  100 us (93%)
  other arithmetic  4.18 us (4%)
  between operations  3.07 us (3%)
    pallas_call x1, Pallas kernels, body(): pl.pallas_call(kernel, out_shape=(jax.ShapeDtypeStruct((COLS, COLS), F32)...  100 us
    add x1, other arithmetic, body(): return (grad_acc + weight_grad, loss)  2.98 us

profile of v3, /device:TPU:1, one launch (start us, length us, event | category | flops | bytes accessed | tf_op | source)
XLA Modules:
  0.0 107.7 jit_solution(15043125510271233048)
XLA Ops:
  1.3 1.2 %pad_maximum_fusion.packed = bf16[3,128,1024]{2,1,0:T(8,128)(2,1)S(1)} fusion(bf16[1,128,1024]{2,1,0:T(8,128)(2,1)} %bitcast.3, bf16[1,128,1024]{2,1,0:T(8,128)(2,1)} %bitcast.4, bf16[1,128,1024]{2,1,0:T(8,128)(2,1)} %bitcast.5), kind=kLoop, calls=%fused_computation | loop fusion | flops 786432 | bytes 1572864 | tf_op jit(solution)/shard_map/stack | solution.py:553
  2.5 0.0 copy-start
  2.5 100.4 %barlow.1 = (f32[1024,1024]{1,0:T(8,128)S(1)}, f32[1]{0:T(128)}) custom-call(bf16[3,128,1024]{2,1,0:T(8,128)(2,1)S(1)} %pad_maximum_fusion.packed, f32[1]{0:T(128)S(6)} %copy.8.scale_ref), custom_call_target="tpu_custom_call" | custom-call | flops 6000000000 | bytes 8000000 | tf_op jit(solution)/shard_map/barlow/pallas_call | solution.py:516
  102.9 0.0 copy-done
  102.9 3.0 %add.3 = f32[1024,1024]{1,0:T(8,128)} add(f32[1024,1024]{1,0:T(8,128)S(1)} %copy-done, f32[1024,1024]{1,0:T(8,128)S(1)} %get-tuple-element.4) | non-fusion elementwise | flops 1048576 | bytes 12582912 | tf_op jit(solution)/shard_map/add | solution.py:554
Async XLA Ops:
  2.5 100.5 %copy-start = (f32[1024,1024]{1,0:T(8,128)S(1)}, f32[1024,1024]{1,0:T(8,128)}, u32[]{:S(2)}) copy-start(f32[1024,1024]{1,0:T(8,128)} %param.8) | copy-start | bytes 12582916

commit v4 on v3

--- a/solution.py
+++ b/solution.py
@@ -222,7 +222,7 @@
 def kernel(
     packed, scale_ref,
     weight, loss_ref,
-    one, two, grad, hid, normed_one, normed_two, fixed, raw, part, part_in, gram, spread, stats, sums, losses,
+    one, two, grad, hid, normed_one, normed_two, fixed, raw, part, part_in, gram, spread, stats, sums, losses, length,
     local_sem, one_s, one_r, two_s, two_r, grad_s, grad_r, hid_s, hid_r,
     part_s, part_r, gram_s, gram_r, stats_s, stats_r, sums_s, sums_r, loss_s, loss_r,
 ):
@@ -283,6 +283,7 @@
     gather_hid.send(0)
     gather_hid.step(0, 0)
     gather_two.stage_b()
+    gather_hid.step(0, 1)
     stats_moves[0][1]()
     centre, inverse = merge_statistics(stats, 0, batch)
 
@@ -313,49 +314,54 @@
         gram[group, feat] = lax.fori_loop(0, PEERS, add, jnp.zeros((HALF, ROWS), F32)).astype(BF)
         gram_moves[group][0]()
 
-    for place, (pair, slot) in enumerate(gather_two.near):
-        gather_two.recv(slot)
-        gram_pair(0, place, pair)
-    part_moves[0][0]()
+    def gram_pairs(group, first, pairs):
+        for place, (pair, slot) in enumerate(pairs):
+            gather_two.recv(slot)
+            gram_pair(group, first + place, pair)
+
+    gram_pairs(0, 0, gather_two.near[:2])
+    gather_two.stage_c()
     gather_hid.recv(0)
     gather_hid.step(1, 0)
-    gather_two.stage_c()
-    gather_two.recv(15)
-    gram_pair(1, 0, gather_two.later[0][0])
-    gather_hid.step(0, 1)
-    add_parts(0)
+    gram_pairs(0, 2, gather_two.near[2:])
+    part_moves[0][0]()
+    gram_pairs(1, 0, gather_two.later[:1])
     gather_two.stage_d()
     gather_one.stage_a()
+    gram_pairs(1, 1, gather_two.later[1:])
+    part_moves[1][0]()
     start_statistics(1, one)
-    for place, (pair, slot) in list(enumerate(gather_two.later))[1:]:
-        gather_two.recv(slot)
-        gram_pair(1, place, pair)
-    part_moves[1][0]()
-    gather_hid.step(1, 1)
+    add_parts(0)
     gather_one.stage_b()
-    add_parts(1)
-    gather_hid.step(0, 2)
-
     stats_moves[1][1]()
     centre_one, inverse_one = merge_statistics(stats, 1, batch)
 
     def norm_pair(pair, acc):
-        def norm(block, rows, acc):
-            values = one[2 * pair + block, rows].astype(F32)
-            normed = ((values - centre_one) * inverse_one).astype(BF)
-            normed_one[2 * pair + block, rows] = normed
-            return acc + fold(
-                normed.astype(F32) * normed_two[2 * pair + block, rows].astype(F32)
-            )
-
-        return over_rows(2, norm, acc)
+        for block in range(2):
+            at = 2 * pair + block
+
+            def norm(i, rows, accs):
+                values = one[at, rows].astype(F32)
+                normed = ((values - centre_one) * inverse_one).astype(BF)
+                normed_one[at, rows] = normed
+                share = normed.astype(F32)
+                return (
+                    accs[0] + fold(share * normed_two[at, rows].astype(F32)),
+                    accs[1] + fold(share * share),
+                )
+
+            acc, norms = over_rows(1, norm, (acc, jnp.zeros((8, COLS), F32)))
+            norms = jnp.sum(norms, axis=0, keepdims=True)
+            length[at] = 1.0 / jnp.maximum(norms, 1e-3)
+        return acc
 
     acc = jnp.zeros((8, COLS), F32)
+    gather_one.stage_c()
     for pair, slot in gather_one.near:
         gather_one.recv(slot)
         acc = norm_pair(pair, acc)
-    gather_one.stage_c()
-    gather_hid.step(1, 2)
+    add_parts(1)
+    gather_hid.step(0, 2)
     gather_one.stage_d()
     for pair, slot in gather_one.later:
         gather_one.recv(slot)
@@ -386,6 +392,7 @@
 
     gram_moves[0][1]()
     add_spread(0, gather_one.near)
+    gather_hid.step(1, 1)
     gram_moves[1][1]()
     add_spread(1, gather_one.later)
     factor = scale * (2.0 * off_weight / batch)
@@ -405,16 +412,16 @@
     accs = over_rows(1, norm_step, (zero, zero, zero))
     sum_grad = jnp.sum(accs[0], axis=0, keepdims=True)
     sum_cross = jnp.sum(accs[1], axis=0, keepdims=True)
-    near_grad = sum_grad / ROWS
-    near_cross = sum_cross / ROWS
+    near_tilt = sum_cross * length[dp]
 
     def grad_step(block, rows, carry):
         share = normed_one[dp, rows].astype(F32)
-        grad[dp, rows] = (spread[rows] - near_grad - share * near_cross).astype(BF)
+        grad[dp, rows] = (spread[rows] - share * near_tilt).astype(BF)
         return carry
 
     over_rows(1, grad_step, 0)
     gather_grad.stage_a()
+    gather_hid.step(0, 3)
     square = jnp.sum(accs[2], axis=0, keepdims=True) / (float(batch) * float(batch))
     terms = off_weight * square + (
         (1.0 - corr) * (1.0 - corr) - off_weight * corr * corr
@@ -430,8 +437,10 @@
         "dp", dp, lambda p: sums.at[dp], sums, sums_s, sums_r
     )
     sums_start()
-    gather_hid.step(0, 3)
     gather_grad.stage_b()
+    gather_hid.step(1, 2)
+    gather_grad.stage_c()
+    gather_hid.step(1, 3)
     sums_recv()
     total = lax.fori_loop(
         0, PEERS, lambda j, acc: acc + sums[j], jnp.zeros((2, COLS + 128), F32)
@@ -441,19 +450,17 @@
         "feat", feat, lambda p: losses.at[feat], losses, loss_s, loss_r
     )
     loss_start()
-    gather_hid.step(1, 3)
     mean_grad = total[0:1, :COLS] / batch
     mean_cross = total[1:2, :COLS] / batch
 
     def fix_pair(pair, place):
         for block in range(2):
             at = 2 * pair + block
-            shift = mean_grad - sums[at, 0:1, :COLS] / ROWS
-            tilt = mean_cross - sums[at, 1:2, :COLS] / ROWS
+            tilt = mean_cross - sums[at, 1:2, :COLS] * length[at]
 
             def fix(i, rows, carry):
                 share = normed_one[at, rows].astype(F32)
-                value = grad[at, rows].astype(F32) - shift - share * tilt
+                value = grad[at, rows].astype(F32) - mean_grad - share * tilt
                 fixed[2 * place + block, rows] = (value * inverse_one).astype(BF)
                 return carry
 
@@ -463,7 +470,7 @@
         count = 2 * len(pairs)
 
         def step(i, carry):
-            rows = pl.ds(pl.multiple_of(i * 512, 512), 512)
+            rows = pl.ds(pl.multiple_of(i * 1024, 1024), 1024)
             lhs = jnp.concatenate(
                 [hid[2 * pair + block, rows] for pair in pairs for block in range(2)], axis=1
             )
@@ -476,7 +483,7 @@
                 weight[rows] += product
             return carry
 
-        lax.fori_loop(0, COLS // 512, step, 0)
+        lax.fori_loop(0, COLS // 1024, step, 0)
 
     def finish_pairs(group, first):
         for place, (pair, slot) in enumerate(group):
@@ -486,10 +493,9 @@
 
     gather_hid.recv(7, 8, 15, 16)
     finish_pairs(gather_grad.near[:2], True)
-    gather_grad.stage_c()
     finish_pairs(gather_grad.near[2:], False)
+    finish_pairs(gather_grad.later[:1], False)
     gather_grad.stage_d()
-    finish_pairs(gather_grad.later[:1], False)
     finish_pairs(gather_grad.later[1:], False)
 
     loss_recv()
@@ -537,6 +543,7 @@
             pltpu.VMEM((2, PEERS, 2, COLS), F32),
             pltpu.VMEM((PEERS, 2, COLS + 128), F32),
             pltpu.VMEM((PEERS, 2, 128), F32),
+            pltpu.VMEM((PEERS, 1, COLS), F32),
             dma((3,)),
         ]
         + [dma, dma((19,))] * 3

time: 108 us -> 101 us (0.935)
  Pallas kernels: 100 us -> 93.3 us
    pallas_call x1, Pallas kernels: 100 us -> 93.3 us  [body(): pl.pallas_call(kernel, out_shape=(jax.ShapeDtypeStruct((COLS, COLS), F32)...]
where the time goes in v4:
time: 101 us
  Pallas kernels  93.3 us (92%)
  other arithmetic  4.18 us (4%)
  between operations  3.07 us (3%)
    pallas_call x1, Pallas kernels, body(): pl.pallas_call(kernel, out_shape=(jax.ShapeDtypeStruct((COLS, COLS), F32)...  93.3 us
    add x1, other arithmetic, body(): return (grad_acc + weight_grad, loss)  2.98 us

profile of v4, /device:TPU:1, one launch (start us, length us, event | category | flops | bytes accessed | tf_op | source)
XLA Modules:
  0.0 100.6 jit_solution(7146076959636741283)
XLA Ops:
  1.3 1.2 %pad_maximum_fusion.packed = bf16[3,128,1024]{2,1,0:T(8,128)(2,1)S(1)} fusion(bf16[1,128,1024]{2,1,0:T(8,128)(2,1)} %bitcast.3, bf16[1,128,1024]{2,1,0:T(8,128)(2,1)} %bitcast.4, bf16[1,128,1024]{2,1,0:T(8,128)(2,1)} %bitcast.5), kind=kLoop, calls=%fused_computation | loop fusion | flops 786432 | bytes 1572864 | tf_op jit(solution)/shard_map/stack | solution.py:560
  2.5 0.0 copy-start
  2.5 93.3 %barlow.1 = (f32[1024,1024]{1,0:T(8,128)S(1)}, f32[1]{0:T(128)}) custom-call(bf16[3,128,1024]{2,1,0:T(8,128)(2,1)S(1)} %pad_maximum_fusion.packed, f32[1]{0:T(128)S(6)} %copy.8.scale_ref), custom_call_target="tpu_custom_call" | custom-call | flops 6000000000 | bytes 8000000 | tf_op jit(solution)/shard_map/barlow/pallas_call | solution.py:522
  95.8 0.0 copy-done
  95.9 3.0 %add.3 = f32[1024,1024]{1,0:T(8,128)} add(f32[1024,1024]{1,0:T(8,128)S(1)} %copy-done, f32[1024,1024]{1,0:T(8,128)S(1)} %get-tuple-element.4) | non-fusion elementwise | flops 1048576 | bytes 12582912 | tf_op jit(solution)/shard_map/add | solution.py:561
Async XLA Ops:
  2.5 93.4 %copy-start = (f32[1024,1024]{1,0:T(8,128)S(1)}, f32[1024,1024]{1,0:T(8,128)}, u32[]{:S(2)}) copy-start(f32[1024,1024]{1,0:T(8,128)} %param.8) | copy-start | bytes 12582916

commit v5 on v4

--- a/solution.py
+++ b/solution.py
@@ -14,6 +14,7 @@
 ROWS = 128
 COLS = 1024
 HALF = ROWS // 2
+PIECE = (48, 32)
 CHUNK = 64
 
 
@@ -160,19 +161,17 @@
         remote(every, every, self.ss, self.rs.at[0], self.any_peer).wait_send()
 
 
-def exchange(axis, me, source, dst, ss, rs):
-    others = dst.at[pl.ds(0, PEERS - 1)]
-
+def exchange(axis, me, source, target, every, ss, rs):
     def start():
         def step(j, carry):
             peer = (me + j) % PEERS
-            remote(source(peer), dst.at[me], ss, rs, {axis: peer}).start()
+            remote(source(peer), target, ss, rs, {axis: peer}).start()
             return carry
 
         lax.fori_loop(1, PEERS, step, 0)
 
     def all_of_them():
-        return remote(others, others, ss, rs, {axis: (me + 1) % PEERS})
+        return remote(every, every, ss, rs, {axis: (me + 1) % PEERS})
 
     return start, lambda: all_of_them().wait_recv(), lambda: all_of_them().wait_send()
 
@@ -222,9 +221,9 @@
 def kernel(
     packed, scale_ref,
     weight, loss_ref,
-    one, two, grad, hid, normed_one, normed_two, fixed, raw, part, part_in, gram, spread, stats, sums, losses, length,
+    one, two, grad, hid, normed_one, normed_two, fixed, raw, part, part_in, gram, spread, stats, sums, losses, length, mirror,
     local_sem, one_s, one_r, two_s, two_r, grad_s, grad_r, hid_s, hid_r,
-    part_s, part_r, gram_s, gram_r, stats_s, stats_r, sums_s, sums_r, loss_s, loss_r,
+    part_s, part_r, gram_s, gram_r, stats_s, stats_r, sums_s, sums_r, loss_s, loss_r, mirror_s, mirror_r,
 ):
     dp, feat = lax.axis_index("dp"), lax.axis_index("feat")
     batch = ROWS * PEERS
@@ -258,15 +257,29 @@
     gather_grad = DpGather(grad, grad_s, grad_r, dp)
     gather_hid = HiddenGather(hid, hid_s, hid_r, feat)
     stats_moves = [
-        exchange("dp", dp, source(k), stats.at[k], stats_s.at[k], stats_r.at[k])
-        for source, k in ((lambda k: lambda p: stats.at[k, dp], v) for v in range(2))
+        exchange(
+            "dp", dp, lambda p, k=k: stats.at[k, dp], stats.at[k, dp],
+            stats.at[k, pl.ds(0, PEERS - 1)], stats_s.at[k], stats_r.at[k],
+        )
+        for k in range(2)
     ]
-    part_moves, gram_moves = [
-        [exchange("feat", feat, source(k), dst.at[k], ss.at[k], rs.at[k]) for k in range(2)]
-        for source, dst, ss, rs in (
-            (lambda k: lambda p: part.at[k, p], part_in, part_s, part_r),
-            (lambda k: lambda p: gram.at[k, feat], gram, gram_s, gram_r),
+    def piece(k, owner):
+        return pl.ds(pl.multiple_of(owner * PIECE[k], 16), PIECE[k])
+
+    part_moves = [
+        exchange(
+            "feat", feat, lambda p, k=k: part.at[k, piece(k, p)],
+            part_in.at[k, feat, pl.ds(0, PIECE[k])],
+            part_in.at[k, pl.ds(0, PEERS - 1), pl.ds(0, PIECE[k])], part_s.at[k], part_r.at[k],
         )
+        for k in range(2)
+    ]
+    gram_moves = [
+        exchange(
+            "feat", feat, lambda p, k=k: gram.at[k, piece(k, feat)], gram.at[k, piece(k, feat)],
+            gram.at[k, pl.ds(0, (PEERS - 1) * PIECE[k])], gram_s.at[k], gram_r.at[k],
+        )
+        for k in range(2)
     ]
     pl.semaphore_wait(barrier, 2 * (PEERS - 1))
 
@@ -287,51 +300,107 @@
     stats_moves[0][1]()
     centre, inverse = merge_statistics(stats, 0, batch)
 
-    def gram_pair(group, place, pair):
+    def norm_two(pair):
         def norm(block, rows, carry):
             values = two[2 * pair + block, rows].astype(F32)
             normed_two[2 * pair + block, rows] = ((values - centre) * inverse).astype(BF)
             return carry
 
         over_rows(2, norm, 0)
+
+    def gram_tiles(group, place, first, count):
         tile = lax.dot_general(
             normed_two[dp],
-            normed_two[pl.ds(2 * pair, 2)].reshape(2 * ROWS, COLS),
+            normed_two[pl.ds(first, count)].reshape(count * ROWS, COLS),
             (((1,), (1,)), ((), ())),
             preferred_element_type=F32,
         ).astype(BF)
-        first = 4 * place
-        part[group, first : first + 2] = tile[:, :ROWS].reshape(2, HALF, ROWS)
-        part[group, first + 2 : first + 4] = tile[:, ROWS:].reshape(2, HALF, ROWS)
+        for k in range(count):
+            rows = pl.ds((place + k) * ROWS, ROWS)
+            part[group, rows] = tile[:, k * ROWS : (k + 1) * ROWS]
 
     def add_parts(group):
-        part_in[group, feat] = part[group, feat]
+        size = PIECE[group]
+        part_in[group, feat, :size] = part[group, piece(group, feat)]
         part_moves[group][1]()
 
         def add(j, acc):
-            return acc + part_in[group, j].astype(F32)
-
-        gram[group, feat] = lax.fori_loop(0, PEERS, add, jnp.zeros((HALF, ROWS), F32)).astype(BF)
+            return acc + part_in[group, j, :size].astype(F32)
+
+        total = lax.fori_loop(0, PEERS, add, jnp.zeros((size, ROWS), F32))
+        gram[group, piece(group, feat)] = total.astype(BF)
         gram_moves[group][0]()
 
-    def gram_pairs(group, first, pairs):
-        for place, (pair, slot) in enumerate(pairs):
-            gather_two.recv(slot)
-            gram_pair(group, first + place, pair)
-
-    gram_pairs(0, 0, gather_two.near[:2])
+    core, y, x = dp % 2, (dp // 2) % 4, dp // 8
+    by_x = jnp.where(x == 0, core, 1 - core)
+    by_y = jnp.where(y < 2, core, 1 - core)
+    pair_of = {
+        name: getattr(gather_two, name) // 2 for name in ("own", "xo", "ym", "yp", "y2", "xm", "xp", "x2")
+    }
+    xo_block, y2_block, x2_block = (
+        2 * pair_of[name] + kept for name, kept in (("xo", by_x), ("y2", by_y), ("x2", by_x))
+    )
+
+    def mirror_copy(group, place, target, slot):
+        return remote(
+            gram.at[group, pl.ds(place * ROWS, ROWS)],
+            mirror.at[group, slot],
+            mirror_s.at[group],
+            mirror_r.at[group],
+            {"dp": target},
+        )
+
+    mirror_sends = (
+        [(2, xo_block, 2), (3, 2 * pair_of["ym"], core), (4, 2 * pair_of["ym"] + 1, core)],
+        [
+            (0, y2_block, 2),
+            (1, 2 * pair_of["xm"], core),
+            (2, 2 * pair_of["xm"] + 1, core),
+            (3, x2_block, 3),
+        ],
+    )
+
+    def mirror_start(group):
+        for place, target, slot in mirror_sends[group]:
+            mirror_copy(group, place, target, slot).start()
+
+    def mirror_all(group):
+        every = mirror.at[group, pl.ds(0, len(mirror_sends[group]))]
+        return remote(every, every, mirror_s.at[group], mirror_r.at[group], {"dp": xo_block})
+
+    part[0, 5 * ROWS :] = jnp.zeros((ROWS, ROWS), BF)
+    gather_two.recv(5)
+    norm_two(pair_of["own"])
+    gram_tiles(0, 0, 2 * pair_of["own"], 2)
+    gather_two.recv(14)
+    norm_two(pair_of["xo"])
+    gram_tiles(0, 2, xo_block, 1)
+    gather_two.recv(12)
+    norm_two(pair_of["ym"])
+    gram_tiles(0, 3, 2 * pair_of["ym"], 2)
+    part_moves[0][0]()
     gather_two.stage_c()
     gather_hid.recv(0)
     gather_hid.step(1, 0)
-    gram_pairs(0, 2, gather_two.near[2:])
-    part_moves[0][0]()
-    gram_pairs(1, 0, gather_two.later[:1])
+    gather_two.recv(13)
+    norm_two(pair_of["yp"])
+    gather_two.recv(15)
+    norm_two(pair_of["y2"])
+    gram_tiles(1, 0, y2_block, 1)
     gather_two.stage_d()
     gather_one.stage_a()
-    gram_pairs(1, 1, gather_two.later[1:])
+    gather_two.recv(16)
+    norm_two(pair_of["xm"])
+    gram_tiles(1, 1, 2 * pair_of["xm"], 2)
+    gather_two.recv(18)
+    norm_two(pair_of["x2"])
+    gram_tiles(1, 3, x2_block, 1)
     part_moves[1][0]()
+    gather_two.recv(17)
+    norm_two(pair_of["xp"])
     start_statistics(1, one)
     add_parts(0)
+    gather_hid.step(0, 2)
     gather_one.stage_b()
     stats_moves[1][1]()
     centre_one, inverse_one = merge_statistics(stats, 1, batch)
@@ -361,8 +430,11 @@
         gather_one.recv(slot)
         acc = norm_pair(pair, acc)
     add_parts(1)
-    gather_hid.step(0, 2)
+    gram_moves[0][1]()
+    mirror_start(0)
+    gather_hid.step(1, 1)
     gather_one.stage_d()
+    gather_hid.step(0, 3)
     for pair, slot in gather_one.later:
         gather_one.recv(slot)
         acc = norm_pair(pair, acc)
@@ -370,31 +442,56 @@
     scale = scale_ref[0] / batch
     weight_diag = scale * (-2.0 * (1.0 - corr) - 2.0 * off_weight * corr)
 
-    def add_spread(group, pairs):
-        for place, (pair, _) in enumerate(pairs):
-            first = 4 * place
-            rows = jnp.concatenate(
-                [
-                    gram[group, first : first + 2].reshape(ROWS, ROWS),
-                    gram[group, first + 2 : first + 4].reshape(ROWS, ROWS),
-                ],
-                axis=1,
-            )
+    def add_spread(group, terms):
+        for k in range(0, len(terms), 2):
+            some = terms[k : k + 2]
             product = jnp.dot(
-                rows,
-                normed_one[pl.ds(2 * pair, 2)].reshape(2 * ROWS, COLS),
+                jnp.concatenate([tile for tile, _ in some], axis=1),
+                jnp.concatenate([normed_one[block] for _, block in some], axis=0),
                 preferred_element_type=F32,
             )
-            if group == 0 and place == 0:
+            if group == 0 and k == 0:
                 spread[...] = product
             else:
                 spread[...] += product
 
-    gram_moves[0][1]()
-    add_spread(0, gather_one.near)
-    gather_hid.step(1, 1)
+    def kept_tile(group, place):
+        return gram[group, place * ROWS : (place + 1) * ROWS]
+
+    def mirrored_tile(group, slot):
+        return mirror[group, slot].T
+
     gram_moves[1][1]()
-    add_spread(1, gather_one.later)
+    mirror_start(1)
+    mirror_all(0).wait_recv()
+    add_spread(
+        0,
+        [
+            (kept_tile(0, 0), 2 * pair_of["own"]),
+            (kept_tile(0, 1), 2 * pair_of["own"] + 1),
+            (kept_tile(0, 2), xo_block),
+            (mirrored_tile(0, 2), 4 * pair_of["xo"] + 1 - xo_block),
+            (kept_tile(0, 3), 2 * pair_of["ym"]),
+            (kept_tile(0, 4), 2 * pair_of["ym"] + 1),
+            (mirrored_tile(0, 0), 2 * pair_of["yp"]),
+            (mirrored_tile(0, 1), 2 * pair_of["yp"] + 1),
+        ],
+    )
+    gather_hid.step(1, 2)
+    mirror_all(1).wait_recv()
+    add_spread(
+        1,
+        [
+            (kept_tile(1, 0), y2_block),
+            (mirrored_tile(1, 2), 4 * pair_of["y2"] + 1 - y2_block),
+            (kept_tile(1, 1), 2 * pair_of["xm"]),
+            (kept_tile(1, 2), 2 * pair_of["xm"] + 1),
+            (mirrored_tile(1, 0), 2 * pair_of["xp"]),
+            (mirrored_tile(1, 1), 2 * pair_of["xp"] + 1),
+            (kept_tile(1, 3), x2_block),
+            (mirrored_tile(1, 3), 4 * pair_of["x2"] + 1 - x2_block),
+        ],
+    )
     factor = scale * (2.0 * off_weight / batch)
     zero = jnp.zeros((8, COLS), F32)
 
@@ -421,7 +518,7 @@
 
     over_rows(1, grad_step, 0)
     gather_grad.stage_a()
-    gather_hid.step(0, 3)
+    gather_hid.step(1, 3)
     square = jnp.sum(accs[2], axis=0, keepdims=True) / (float(batch) * float(batch))
     terms = off_weight * square + (
         (1.0 - corr) * (1.0 - corr) - off_weight * corr * corr
@@ -434,20 +531,19 @@
     sums[dp, 0:1, COLS:] = lanes
     sums[dp, 1:2, COLS:] = jnp.zeros_like(lanes)
     sums_start, sums_recv, sums_send = exchange(
-        "dp", dp, lambda p: sums.at[dp], sums, sums_s, sums_r
+        "dp", dp, lambda p: sums.at[dp], sums.at[dp], sums.at[pl.ds(0, PEERS - 1)], sums_s, sums_r
     )
     sums_start()
     gather_grad.stage_b()
-    gather_hid.step(1, 2)
     gather_grad.stage_c()
-    gather_hid.step(1, 3)
     sums_recv()
     total = lax.fori_loop(
         0, PEERS, lambda j, acc: acc + sums[j], jnp.zeros((2, COLS + 128), F32)
     )
     losses[feat] = total[:, COLS:]
     loss_start, loss_recv, loss_send = exchange(
-        "feat", feat, lambda p: losses.at[feat], losses, loss_s, loss_r
+        "feat", feat, lambda p: losses.at[feat], losses.at[feat],
+        losses.at[pl.ds(0, PEERS - 1)], loss_s, loss_r,
     )
     loss_start()
     mean_grad = total[0:1, :COLS] / batch
@@ -511,6 +607,7 @@
         stats_moves[group][2]()
         part_moves[group][2]()
         gram_moves[group][2]()
+        mirror_all(group).wait_send()
     sums_send()
     loss_send()
 
@@ -536,20 +633,22 @@
             pltpu.VMEM((PEERS, ROWS, COLS), BF),
             pltpu.VMEM((6, ROWS, COLS), BF),
             pltpu.VMEM((ROWS, COLS), BF),
-            pltpu.VMEM((2, PEERS, HALF, ROWS), BF),
-            pltpu.VMEM((2, PEERS, HALF, ROWS), BF),
-            pltpu.VMEM((2, PEERS, HALF, ROWS), BF),
+            pltpu.VMEM((2, 6 * ROWS, ROWS), BF),
+            pltpu.VMEM((2, PEERS, PIECE[0], ROWS), BF),
+            pltpu.VMEM((2, 6 * ROWS, ROWS), BF),
             pltpu.VMEM((ROWS, COLS), F32),
             pltpu.VMEM((2, PEERS, 2, COLS), F32),
             pltpu.VMEM((PEERS, 2, COLS + 128), F32),
             pltpu.VMEM((PEERS, 2, 128), F32),
             pltpu.VMEM((PEERS, 1, COLS), F32),
+            pltpu.VMEM((2, 4, ROWS, ROWS), BF),
             dma((3,)),
         ]
         + [dma, dma((19,))] * 3
         + [dma, dma((17,))]
         + [dma((2,))] * 6
-        + [dma] * 4,
+        + [dma] * 4
+        + [dma((2,))] * 2,
         compiler_params=pltpu.CompilerParams(
             collective_id=0, has_side_effects=True, vmem_limit_bytes=48 << 20
         ),

time: 101 us -> 98.6 us (0.976)
  Pallas kernels: 93.3 us -> 91.2 us
    pallas_call x1, Pallas kernels: 93.3 us -> 91.2 us  [body(): pl.pallas_call(kernel, out_shape=(jax.ShapeDtypeStruct((COLS, COLS), F32)...]
where the time goes in v5:
time: 98.6 us; the launch traced here: 98.5 us
  Pallas kernels  91.2 us (92%)
  other arithmetic  4.18 us (4%)
  between operations  3.07 us (3%)
    pallas_call x1, Pallas kernels, body(): pl.pallas_call(kernel, out_shape=(jax.ShapeDtypeStruct((COLS, COLS), F32)...  91.2 us
    add x1, other arithmetic, body(): return (grad_acc + weight_grad, loss)  2.98 us

profile of v5, /device:TPU:1, one launch (start us, length us, event | category | flops | bytes accessed | tf_op | source)
XLA Modules:
  0.0 98.5 jit_solution(2283100900738663241)
XLA Ops:
  1.3 1.2 %pad_maximum_fusion.packed = bf16[3,128,1024]{2,1,0:T(8,128)(2,1)S(1)} fusion(bf16[1,128,1024]{2,1,0:T(8,128)(2,1)} %bitcast.3, bf16[1,128,1024]{2,1,0:T(8,128)(2,1)} %bitcast.4, bf16[1,128,1024]{2,1,0:T(8,128)(2,1)} %bitcast.5), kind=kLoop, calls=%fused_computation | loop fusion | flops 786432 | bytes 1572864 | tf_op jit(solution)/shard_map/stack | solution.py:659
  2.5 0.0 copy-start
  2.5 91.2 %barlow.1 = (f32[1024,1024]{1,0:T(8,128)S(1)}, f32[1]{0:T(128)}) custom-call(bf16[3,128,1024]{2,1,0:T(8,128)(2,1)S(1)} %pad_maximum_fusion.packed, f32[1]{0:T(128)S(6)} %copy.8.scale_ref), custom_call_target="tpu_custom_call" | custom-call | flops 6000000000 | bytes 8000000 | tf_op jit(solution)/shard_map/barlow/pallas_call | solution.py:619
  93.7 0.0 copy-done
  93.7 3.0 %add.3 = f32[1024,1024]{1,0:T(8,128)} add(f32[1024,1024]{1,0:T(8,128)S(1)} %copy-done, f32[1024,1024]{1,0:T(8,128)S(1)} %get-tuple-element.4) | non-fusion elementwise | flops 1048576 | bytes 12582912 | tf_op jit(solution)/shard_map/add | solution.py:660
Async XLA Ops:
  2.5 91.2 %copy-start = (f32[1024,1024]{1,0:T(8,128)S(1)}, f32[1024,1024]{1,0:T(8,128)}, u32[]{:S(2)}) copy-start(f32[1024,1024]{1,0:T(8,128)} %param.8) | copy-start | bytes 12582916

commit v6 on v5

--- a/solution.py
+++ b/solution.py
@@ -219,7 +219,7 @@
 
 
 def kernel(
-    packed, scale_ref,
+    packed, scale_ref, grad_acc,
     weight, loss_ref,
     one, two, grad, hid, normed_one, normed_two, fixed, raw, part, part_in, gram, spread, stats, sums, losses, length, mirror,
     local_sem, one_s, one_r, two_s, two_r, grad_s, grad_r, hid_s, hid_r,
@@ -234,6 +234,8 @@
         pltpu.make_async_copy(packed.at[1], one.at[dp], local_sem.at[1]),
         pltpu.make_async_copy(packed.at[2], raw, local_sem.at[2]),
     ]
+    base = pltpu.make_async_copy(grad_acc, weight, local_sem.at[3])
+    base.start()
     for copy in local:
         copy.start()
 
@@ -574,7 +576,7 @@
                 lhs, fixed[:count].reshape(count * ROWS, COLS), preferred_element_type=F32
             )
             if first:
-                weight[rows] = product
+                weight[rows] += product
             else:
                 weight[rows] += product
             return carry
@@ -588,6 +590,7 @@
         add_pairs([pair for pair, _ in group], first)
 
     gather_hid.recv(7, 8, 15, 16)
+    base.wait()
     finish_pairs(gather_grad.near[:2], True)
     finish_pairs(gather_grad.near[2:], False)
     finish_pairs(gather_grad.later[:1], False)
@@ -622,7 +625,7 @@
             jax.ShapeDtypeStruct((COLS, COLS), F32),
             jax.ShapeDtypeStruct((1,), F32),
         ),
-        in_specs=[in_hbm, in_smem],
+        in_specs=[in_hbm, in_smem, in_hbm],
         out_specs=(pl.BlockSpec(memory_space=pltpu.VMEM), in_smem),
         scratch_shapes=[
             pltpu.VMEM((PEERS, ROWS, COLS), BF),
@@ -642,7 +645,7 @@
             pltpu.VMEM((PEERS, 2, 128), F32),
             pltpu.VMEM((PEERS, 1, COLS), F32),
             pltpu.VMEM((2, 4, ROWS, ROWS), BF),
-            dma((3,)),
+            dma((4,)),
         ]
         + [dma, dma((19,))] * 3
         + [dma, dma((17,))]
@@ -656,8 +659,8 @@
             flops=6 * 10**9, bytes_accessed=8 * 10**6, transcendentals=0
         ),
         name="barlow",
-    )(jnp.stack([z_two, z_one, hidden_in]), loss_scale)
-    return grad_acc + weight_grad, loss
+    )(jnp.stack([z_two, z_one, hidden_in]), loss_scale, grad_acc)
+    return weight_grad, loss
 
 
 def solution(mesh):

time: 98.6 us -> 97.5 us (0.989)
  other arithmetic: 4.18 us -> 1.2 us
  local copies, waits for them, and re-layouts: 0.01 us -> 2.02 us
    add x1 -> x0, other arithmetic: 2.98 us -> none  [body(): return (grad_acc + weight_grad, loss)]
    unnamed x2 -> x1, local copies, waits for them, and re-layouts: 0.01 us -> 2.02 us
where the time goes in v6:
time: 97.5 us; the launch traced here: 97.4 us
  Pallas kernels  91.2 us (94%)
  between operations  2.98 us (3%)
  local copies, waits for them, and re-layouts  2.02 us (2%)
  other arithmetic  1.2 us (1%)
    pallas_call x1, Pallas kernels, body(): pl.pallas_call(kernel, out_shape=(jax.ShapeDtypeStruct((COLS, COLS), F32)...  91.2 us
    unnamed x1, local copies, waits for them, and re-layouts  2.02 us

profile of v6, /device:TPU:1, one launch (start us, length us, event | category | flops | bytes accessed | tf_op | source)
XLA Modules:
  0.0 97.4 jit_solution(18322708735345769313)
XLA Ops:
  1.3 1.2 %pad_maximum_fusion.packed = bf16[3,128,1024]{2,1,0:T(8,128)(2,1)S(1)} fusion(bf16[1,128,1024]{2,1,0:T(8,128)(2,1)} %bitcast.3, bf16[1,128,1024]{2,1,0:T(8,128)(2,1)} %bitcast.4, bf16[1,128,1024]{2,1,0:T(8,128)(2,1)} %bitcast.5), kind=kLoop, calls=%fused_computation | loop fusion | flops 786432 | bytes 1572864 | tf_op jit(solution)/shard_map/stack | solution.py:662
  2.5 91.2 %barlow.1 = (f32[1024,1024]{1,0:T(8,128)S(1)}, f32[1]{0:T(128)}) custom-call(bf16[3,128,1024]{2,1,0:T(8,128)(2,1)S(1)} %pad_maximum_fusion.packed, f32[1]{0:T(128)S(6)} %copy.9.scale_ref, f32[1024,1024]{1,0:T(8,128)} %grad_acc.1), custom_call_target="tpu_custom_call" | custom-call | flops 6000000000 | bytes 8000000 | tf_op jit(solution)/shard_map/barlow/pallas_call | solution.py:622
  93.7 2.0 %copy.10 = f32[1024,1024]{1,0:T(8,128)} copy(f32[1024,1024]{1,0:T(8,128)S(1)} %get-tuple-element.4) | data formatting | bytes 8388608

commit v7 on v6

--- a/solution.py
+++ b/solution.py
@@ -219,7 +219,7 @@
 
 
 def kernel(
-    packed, scale_ref, grad_acc,
+    z_two, z_one, hidden, scale_ref, grad_acc,
     weight, loss_ref,
     one, two, grad, hid, normed_one, normed_two, fixed, raw, part, part_in, gram, spread, stats, sums, losses, length, mirror,
     local_sem, one_s, one_r, two_s, two_r, grad_s, grad_r, hid_s, hid_r,
@@ -230,9 +230,9 @@
     width = COLS * PEERS
 
     local = [
-        pltpu.make_async_copy(packed.at[0], two.at[dp], local_sem.at[0]),
-        pltpu.make_async_copy(packed.at[1], one.at[dp], local_sem.at[1]),
-        pltpu.make_async_copy(packed.at[2], raw, local_sem.at[2]),
+        pltpu.make_async_copy(z_two, two.at[dp], local_sem.at[0]),
+        pltpu.make_async_copy(z_one, one.at[dp], local_sem.at[1]),
+        pltpu.make_async_copy(hidden, raw, local_sem.at[2]),
     ]
     base = pltpu.make_async_copy(grad_acc, weight, local_sem.at[3])
     base.start()
@@ -625,7 +625,7 @@
             jax.ShapeDtypeStruct((COLS, COLS), F32),
             jax.ShapeDtypeStruct((1,), F32),
         ),
-        in_specs=[in_hbm, in_smem, in_hbm],
+        in_specs=[in_hbm, in_hbm, in_hbm, in_smem, in_hbm],
         out_specs=(pl.BlockSpec(memory_space=pltpu.VMEM), in_smem),
         scratch_shapes=[
             pltpu.VMEM((PEERS, ROWS, COLS), BF),
@@ -659,7 +659,7 @@
             flops=6 * 10**9, bytes_accessed=8 * 10**6, transcendentals=0
         ),
         name="barlow",
-    )(jnp.stack([z_two, z_one, hidden_in]), loss_scale, grad_acc)
+    )(*(pltpu.with_memory_space_constraint(v, pltpu.HBM) for v in (z_two, z_one, hidden_in)), loss_scale, grad_acc)
     return weight_grad, loss
 
 

time: 97.5 us -> 96.3 us (0.988)
  other arithmetic: 1.2 us -> 0 us
    another operation x1 -> x0, other arithmetic: 1.2 us -> none  [body(): jnp.stack([z_two, z_one, hidden_in])]
where the time goes in v7:
time: 96.3 us; the launch traced here: 96.2 us
  Pallas kernels  91.2 us (95%)
  between operations  2.97 us (3%)
  local copies, waits for them, and re-layouts  2.02 us (2%)
    pallas_call x1, Pallas kernels, body(): pl.pallas_call(kernel, out_shape=(jax.ShapeDtypeStruct((COLS, COLS), F32)...  91.2 us
    unnamed x1, local copies, waits for them, and re-layouts  2.02 us

profile of v7, /device:TPU:1, one launch (start us, length us, event | category | flops | bytes accessed | tf_op | source)
XLA Modules:
  0.0 96.2 jit_solution(16490433638885447519)
XLA Ops:
  1.3 91.2 %barlow.1 = (f32[1024,1024]{1,0:T(8,128)S(1)}, f32[1]{0:T(128)}) custom-call(bf16[128,1024]{1,0:T(8,128)(2,1)} %z_two.1, bf16[128,1024]{1,0:T(8,128)(2,1)} %z_one.1, bf16[128,1024]{1,0:T(8,128)(2,1)} %hidden.1, f32[1]{0:T(128)S(6)} %copy.9.scale_ref, f32[1024,1024]{1,0:T(8,128)} %grad_acc.1), custom_call_target="tpu_custom_call" | custom-call | flops 6000000000 | bytes 8000000 | tf_op jit(solution)/shard_map/barlow/pallas_call | solution.py:622
  92.4 2.0 %copy.10 = f32[1024,1024]{1,0:T(8,128)} copy(f32[1024,1024]{1,0:T(8,128)S(1)} %get-tuple-element.4) | data formatting | bytes 8388608
